TPU v7x, 32 devices: a whole 2x2x4 slice. The times are simulated.
32 devices in a mesh: groups: 2 (over x), expert: 8 (over z, y), narrow: 2 (over core).
Axes of the slice: x: 2, y: 2, z: 4, core: 2. Of those that a mesh axis runs over, the one named last changes fastest.
Arguments:
- tokens: bfloat16 [128, 5120], P(('groups', 'expert', 'narrow')), parts along dimension 0, may hold values from -6 to 6
- expert_ids: int32 [128], P(('groups', 'expert', 'narrow')), parts along dimension 0, may hold values from 0 to 2, as said below
- replica_plan: int32 [128], P(('groups', 'expert', 'narrow')), parts along dimension 0, may hold values from 0 to 1, as said below
- route_gate: bfloat16 [128], P(('groups', 'expert', 'narrow')), parts along dimension 0, may hold values from 0.099609375 to 1
- capacity: int32 [4], P(('groups', 'narrow')), parts along dimension 0, may hold values from 16 to 32, as said below
- cold_gate_up: bfloat16 [2, 5120, 2, 4096], P('narrow', None, None, 'expert'), may hold values from -0.078125 to 0.078125
- cold_down: bfloat16 [2, 4096, 5120], P('narrow', 'expert'), may hold values from -0.09375 to 0.09375
- hot_gate_up: bfloat16 [5120, 2, 4096], P(None, None, 'expert'), may hold values from -0.078125 to 0.078125
- hot_down: bfloat16 [4096, 5120], P('expert'), may hold values from -0.09375 to 0.09375
- shared_gate_up: bfloat16 [5120, 2, 8192], P(None, None, ('expert', 'narrow')), may hold values from -0.078125 to 0.078125
- shared_down: bfloat16 [8192, 5120], P(('expert', 'narrow')), may hold values from -0.0625 to 0.0625
Outputs:
- mixed: bfloat16 [128, 5120], P(('groups', 'expert', 'narrow')), parts along dimension 0
There are 2 independent parts, one for each index of `groups`. A program takes and returns all parts, laid end to end along the dimension named above; an argument that names none is the same for every part. Nothing has to cross between parts.
Inputs may be any that keep to these rules, and one draw needn't show every extreme that they name: `expert_ids`: the value 2 names the replicated expert; of one device's tokens at most 3 have the same dest, and every device has a dest with exactly 3. `replica_plan`: read only for tokens of expert 2. `capacity`: some instance has exactly 32, and 32 or more tokens have it as dest.
All inputs are finite; a program needn't handle non-finite values.
Results may differ from a plain program's by a relative error of at most 0.0048.
Values may be sent and summed in bfloat16 or wider, within the bound.
No kernel may reach another device: no remote copies, remote signals or barrier semaphores. Data moves between devices by JAX's collectives and lax.ppermute only.
A program may use at most 192 MiB of HBM per device.

v0:
```python
import jax
import jax.numpy as jnp
from jax import lax
from jax.sharding import PartitionSpec as P

SEND = 3


def expert_partial(packed, packed_hot, hot_gate_up, hot_down, cold_gate_up, cold_down):
    width = packed.shape[1]
    part_width = hot_down.shape[0]
    warm_in = jnp.dot(
        packed, hot_gate_up.reshape(width, 2 * part_width), preferred_element_type=jnp.float32
    )
    cold_in = jnp.dot(
        packed, cold_gate_up[0].reshape(width, 2 * part_width), preferred_element_type=jnp.float32
    )
    warm_hidden = jnp.where(
        packed_hot[:, None], jax.nn.silu(warm_in[:, :part_width]) * warm_in[:, part_width:], 0.0
    ).astype(jnp.bfloat16)
    cold_hidden = jnp.where(
        packed_hot[:, None], 0.0, jax.nn.silu(cold_in[:, :part_width]) * cold_in[:, part_width:]
    ).astype(jnp.bfloat16)
    warm_out = jnp.dot(warm_hidden, hot_down, preferred_element_type=jnp.float32)
    return warm_out + jnp.dot(cold_hidden, cold_down[0], preferred_element_type=jnp.float32)


def shared_hidden_rows(rows, shared_gate_up):
    width = rows.shape[1]
    part_width = shared_gate_up.shape[2]
    shared_in = jnp.dot(
        rows, shared_gate_up.reshape(width, 2 * part_width), preferred_element_type=jnp.float32
    )
    return (jax.nn.silu(shared_in[:, :part_width]) * shared_in[:, part_width:]).astype(jnp.bfloat16)


def pick_rows(spots, partial_value):
    taken = jnp.take(partial_value, jnp.maximum(spots, 0), axis=0)
    return jnp.where(spots[:, None] >= 0, taken, 0.0)


def shared_apart(tokens, shared_gate_up, shared_down):
    shared_hidden = shared_hidden_rows(
        lax.all_gather(tokens, ("expert", "narrow"), axis=0, tiled=True), shared_gate_up
    )
    return lax.psum_scatter(
        jnp.dot(shared_hidden, shared_down, preferred_element_type=jnp.float32),
        ("expert", "narrow"),
        scatter_dimension=0,
        tiled=True,
    )


def body(
    tokens,
    expert_ids,
    replica_plan,
    route_gate,
    capacity,
    cold_gate_up,
    cold_down,
    hot_gate_up,
    hot_down,
    shared_gate_up,
    shared_down,
):
    tok_rows, width = tokens.shape
    outer = lax.axis_size("expert")
    inner = lax.axis_size("narrow")
    slots = outer * inner
    cap_rows = tok_rows * slots // inner
    hot = expert_ids == inner
    dest = jnp.where(hot, replica_plan, expert_ids)
    places = inner * SEND
    onehot = (dest[:, None] == jnp.arange(inner, dtype=jnp.int32)[None, :]).astype(jnp.int32)
    position = jnp.sum((jnp.cumsum(onehot, axis=0) - 1) * onehot, axis=1)
    place = dest * SEND + position
    place_match = jnp.arange(places, dtype=jnp.int32)[:, None] == place[None, :]
    send_rows = jnp.dot(
        place_match.astype(jnp.bfloat16), tokens, preferred_element_type=jnp.float32
    ).astype(jnp.bfloat16)
    kind = jnp.where(hot, 2, 1).astype(jnp.int32)
    send_kind = jnp.sum(jnp.where(place_match, kind[None, :], 0), axis=1)
    arrived, arrived_kind = (
        lax.all_to_all(
            send_rows.reshape(inner, SEND, width), "narrow", split_axis=0, concat_axis=0, tiled=True
        ),
        lax.all_to_all(
            send_kind.reshape(inner, SEND), "narrow", split_axis=0, concat_axis=0, tiled=True
        ),
    )
    arrived = arrived.reshape(places, width)
    arrived_kind = arrived_kind.reshape(places)
    live = arrived_kind > 0
    local_rank = jnp.cumsum(live.astype(jnp.int32)) - 1
    count = jnp.sum(live.astype(jnp.int32)).reshape(1)
    counts = lax.all_gather(count, "expert", axis=0, tiled=True)
    offset = jnp.sum(
        jnp.where(jnp.arange(outer, dtype=jnp.int32) < lax.axis_index("expert"), counts, 0)
    )
    position_all = offset + local_rank
    slot_pos = jnp.where(live & (position_all < capacity[0]), position_all, -1)
    arrived_hot = (arrived_kind == 2).astype(jnp.bfloat16)
    start_carry = (
        jnp.zeros((cap_rows, width), jnp.float32),
        jnp.zeros((cap_rows,), jnp.float32),
        jnp.full((slots * SEND,), -1, jnp.int32),
    )
    rows = lax.all_gather(arrived, "expert", axis=0, tiled=True)
    spots = lax.all_gather(slot_pos, "expert", axis=0, tiled=True)
    flags = lax.all_gather(arrived_hot, "expert", axis=0, tiled=True)
    selecting = (spots[None, :] == jnp.arange(cap_rows, dtype=jnp.int32)[:, None]).astype(
        jnp.bfloat16
    )
    packed_sum = jnp.dot(selecting, rows, preferred_element_type=jnp.float32)
    hot_sum = jnp.dot(selecting, flags, preferred_element_type=jnp.float32)
    collect_spots_all = lax.dynamic_update_slice_in_dim(start_carry[2], spots, jnp.int32(0), 0)
    packed_sum, hot_sum, spots_all = (packed_sum, hot_sum, collect_spots_all)
    packed = packed_sum.astype(jnp.bfloat16)
    partial_value = expert_partial(
        packed, hot_sum > 0.5, hot_gate_up, hot_down, cold_gate_up, cold_down
    )
    spots = spots_all
    summed = lax.psum_scatter(
        pick_rows(spots, partial_value), "expert", scatter_dimension=0, tiled=True
    )
    returned = lax.all_to_all(
        summed.reshape(inner, SEND, width), "narrow", split_axis=0, concat_axis=0, tiled=True
    )
    routed = jnp.take(returned.reshape(places, width), place, axis=0)
    shared = shared_apart(tokens, shared_gate_up, shared_down)
    return (shared + route_gate.astype(jnp.float32)[:, None] * routed).astype(jnp.bfloat16)


def solution(mesh):
    in_specs = (
        P(("groups", "expert", "narrow"), None),
        P(("groups", "expert", "narrow")),
        P(("groups", "expert", "narrow")),
        P(("groups", "expert", "narrow")),
        P(("groups", "narrow")),
        P("narrow", None, None, "expert"),
        P("narrow", "expert", None),
        P(None, None, "expert"),
        P("expert", None),
        P(None, None, ("expert", "narrow")),
        P(("expert", "narrow"), None),
    )
    out_specs = P(("groups", "expert", "narrow"), None)
    return jax.shard_map(body, mesh=mesh, in_specs=in_specs, out_specs=out_specs, check_vma=False)
```

profile of v0, /device:TPU:0, one launch (start us, length us, event | category | flops | bytes accessed | tf_op | source)
XLA Modules:
  0.0 304.6 jit_solution(2038708459585585323)
XLA Ops:
  6.5 0.7 compare_select_fusion.1
  7.2 0.2 reduce_window_sum.18
  7.4 0.1 select_reduce_fusion
  7.5 0.6 all_to_all.12
  8.2 3.2 %all-to-all-start = ((s32[2,1,3]{2,1,0:T(1,128)}), s32[2,1,3]{2,1,0:T(1,128)S(1)}, u32[]{:S(2)}, u32[]{:S(2)}) async-start(s32[2,1,3]{2,1,0:T(1,128)} %bitcast.1), calls=%async_computation | async-start | bytes 2048 | tf_op jit(solution)/shard_map/all_to_all | solution.py:88
  12.0 1.1 convolution_convert_fusion.1
  13.1 0.7 reshape.96
  13.8 0.0 all-to-all-done
  13.8 3.3 %all-to-all-start.1 = ((bf16[2,3,5120]{2,1,0:T(4,128)(2,1)}), bf16[2,3,5120]{2,1,0:T(4,128)(2,1)S(1)}, u32[]{:S(2)}, u32[]{:S(2)}) async-start(bf16[2,3,5120]{2,1,0:T(4,128)(2,1)} %reshape.96), calls=%async_computation.1 | async-start | bytes 163840 | tf_op jit(solution)/shard_map/all_to_all | solution.py:85
  17.1 0.0 all-reduce.8.cloned.1.call-start
  17.2 0.1 reshape.127
  17.3 0.1 gt.23
  17.4 0.7 fusion.27
  18.1 0.1 reshape.101
  18.2 1.3 fusion.36
  20.2 1.4 dynamic-update-slice
  21.6 0.2 reduce-window.9
  21.8 13.1 %all-reduce = s32[8]{0:T(128)S(1)} all-reduce(s32[8]{0:T(128)S(1)} %dynamic-update-slice), channel_id=1, replica_groups=mesh['groups'=2,'expert'=8,'narrow'=2] {'expert'}, use_global_device_ids=true, to_apply=%add | all-reduce | flops 8 | bytes 64
  34.9 0.6 fusion.28
  35.5 0.7 fusion.29
  36.2 7.8 %all-reduce.1 = s32[48]{0:T(128)S(1)} all-reduce(s32[48]{0:T(128)S(1)} %fusion.29), channel_id=1, replica_groups=mesh['groups'=2,'expert'=8,'narrow'=2] {'expert'}, use_global_device_ids=true, to_apply=%add.1 | all-reduce | flops 48 | bytes 384
  44.0 0.2 dynamic-update-slice.2
  44.2 22.2 %all-reduce.2 = bf16[48]{0:T(256)(128)(2,1)S(1)} all-reduce(bf16[48]{0:T(256)(128)(2,1)S(1)} %dynamic-update-slice.2), channel_id=1, replica_groups=mesh['groups'=2,'expert'=8,'narrow'=2] {'expert'}, use_global_device_ids=true, to_apply=%add.2 | all-reduce | flops 48 | bytes 192
  66.4 0.1 fusion.2
  66.5 0.0 all-to-all-done.1
  66.6 0.1 reshape.132
  66.6 31.5 %all-gather.1 = bf16[8,6,5120]{2,1,0:T(8,128)(2,1)S(1)} all-gather(bf16[1,6,5120]{2,1,0:T(8,128)(2,1)S(1)} %reshape.132), channel_id=1, replica_groups=mesh['groups'=2,'expert'=8,'narrow'=2] {'expert'}, dimensions={0}, use_global_device_ids=true | all-gather | bytes 552960 | tf_op jit(solution)/shard_map/all_gather | solution.py:109
  98.2 0.2 reshape.133
  98.3 0.2 convolution_convert_fusion
  98.6 11.2 %copy.17 = bf16[640,8,2,512]{3,1,2,0:T(8,128)(2,1)} copy(bf16[640,8,2,512]{3,2,1,0:T(2,128)(2,1)} %bitcast.43) | data formatting | bytes 20971520
  109.8 11.3 %copy.16 = bf16[640,8,2,512]{3,1,2,0:T(8,128)(2,1)} copy(bf16[640,8,2,512]{3,2,1,0:T(2,128)(2,1)} %bitcast.44) | data formatting | bytes 20971520
  121.1 6.0 %fusion.39 = f32[32,1024]{1,0:T(8,128)S(1)} fusion(bf16[32,5120]{1,0:T(8,128)(2,1)S(1)} %convolution_convert_fusion, bf16[5120,1024]{1,0:T(8,128)(2,1)} %bitcast.41), kind=kOutput, calls=%fused_computation.67 | convolution fusion | flops 335544320 | bytes 10944512 | tf_op jit(solution)/shard_map/dot_general | solution.py:15
  127.1 0.9 copy-done
  128.0 1.9 fusion.38
  130.0 0.0 slice-done
  130.0 0.9 slice-done.1
  130.9 1.0 fusion.12
  131.9 0.0 slice-done.3
  132.0 1.1 convolution_add_fusion
  133.0 0.0 copy-start.1
  133.0 0.9 gather_fusion
  133.9 0.3 select_select_fusion
  134.3 23.7 %fusion = f32[8,5120]{1,0:T(8,128)S(1)} fusion(f32[48,5120]{1,0:T(8,128)S(1)} %select_select_fusion), kind=kCustom, calls=%all-reduce-scatter | all-reduce-scatter fusion | flops 327681 | bytes 1147392
  158.0 2.2 collective-permute-start
  160.3 1.9 collective-permute-start.1
  162.1 20.9 %all-gather = bf16[16,4,5120]{2,1,0:T(4,128)(2,1)S(1)} all-gather(bf16[1,4,5120]{2,1,0:T(4,128)(2,1)S(1)} %bitcast.50), channel_id=1, replica_groups=mesh['groups'=2,'expert'=8,'narrow'=2] {'expert','narrow'}, dimensions={0}, use_global_device_ids=true | all-gather | bytes 696320 | tf_op jit(solution)/shard_map/all_gather | solution.py:44
  183.0 0.1 reshape.131
  183.2 11.3 %copy.15 = bf16[640,8,2,512]{3,1,2,0:T(8,128)(2,1)} copy(bf16[640,8,2,512]{3,2,1,0:T(2,128)(2,1)} %bitcast.45) | data formatting | bytes 20971520
  194.5 5.9 %fusion.37 = f32[64,1024]{1,0:T(8,128)S(1)} fusion(bf16[64,5120]{1,0:T(8,128)(2,1)S(1)} %reshape.131, bf16[5120,1024]{1,0:T(8,128)(2,1)} %bitcast.42), kind=kOutput, calls=%fused_computation.65 | convolution fusion | flops 671088640 | bytes 11403264 | tf_op jit(solution)/shard_map/dot_general | solution.py:31
  200.4 0.0 copy-start.2
  200.5 0.0 copy-start.3
  200.5 4.6 %fusion.5 = f32[64,5120]{1,0:T(8,128)} fusion(bf16[512,5120]{1,0:T(8,128)(2,1)} %param.21, f32[64,1024]{1,0:T(8,128)S(1)} %fusion.37), kind=kOutput, calls=%fused_computation.13 | convolution fusion | flops 335740928 | bytes 6815744 | tf_op jit(solution)/shard_map/dot_general | solution.py:47
  205.1 0.0 all-reduce.8.cloned.1.call-update
  205.1 0.0 copy-done.3
  205.1 0.6 dynamic-slice.3
  207.0 0.0 collective-permute-done.1
  207.0 0.0 collective-permute-done
  207.0 0.5 concatenate
  207.6 0.1 reshape.99
  207.7 3.9 %all_to_all.19 = f32[2,3,5120]{2,1,0:T(4,128)S(1)} all-to-all(f32[2,3,5120]{2,1,0:T(4,128)S(1)} %reshape.99), channel_id=1, replica_groups=mesh['groups'=2,'expert'=8,'narrow'=2] {'narrow'}, dimensions={0} | all-to-all | bytes 245760 | tf_op jit(solution)/shard_map/all_to_all | solution.py:127
  211.5 0.1 reshape.100
  211.6 0.6 gather_fusion.1
  212.2 83.9 %all-reduce.8.cloned.1.call-done = f32[64,5120]{1,0:T(8,128)} async-done(((f32[64,5120]{1,0:T(8,128)}), f32[64,5120]{1,0:T(8,128)}) %all-reduce.8.cloned.1.call-update) | async-done | bytes 1310736
  296.1 1.6 fusion.4
  (26 shorter events, 0.2 us)
Async XLA Ops:
  8.2 5.6 %all-to-all-start = ((s32[2,1,3]{2,1,0:T(1,128)}), s32[2,1,3]{2,1,0:T(1,128)S(1)}, u32[]{:S(2)}, u32[]{:S(2)}) async-start(s32[2,1,3]{2,1,0:T(1,128)} %bitcast.1), calls=%async_computation | async-start | bytes 2048 | tf_op jit(solution)/shard_map/all_to_all | solution.py:88
  13.8 52.8 %all-to-all-start.1 = ((bf16[2,3,5120]{2,1,0:T(4,128)(2,1)}), bf16[2,3,5120]{2,1,0:T(4,128)(2,1)S(1)}, u32[]{:S(2)}, u32[]{:S(2)}) async-start(bf16[2,3,5120]{2,1,0:T(4,128)(2,1)} %reshape.96), calls=%async_computation.1 | async-start | bytes 163840 | tf_op jit(solution)/shard_map/all_to_all | solution.py:85
  17.1 279.0 %all-reduce.8.cloned.1.call-start = ((), (), s32[]{:S(2)}) async-start(), calls=%async_computation.3 | async-start | bytes 2621440
  121.1 7.0 %copy-start = (bf16[640,8,2,512]{3,1,2,0:T(8,128)(2,1)S(1)}, bf16[640,8,2,512]{3,1,2,0:T(8,128)(2,1)}, u32[]{:S(2)}) copy-start(bf16[640,8,2,512]{3,1,2,0:T(8,128)(2,1)} %copy.16) | copy-start | bytes 31457284
  121.1 8.9 %slice-start = ((s8[5242880]{0:T(1024)(128)(4,1)}), s8[4194304]{0:T(1024)(128)(4,1)S(1)}, s32[]{:S(2)}) async-start(s8[5242880]{0:T(1024)(128)(4,1)} %bitcast.46), calls=%async_computation.4 | async-start | bytes 8388608
  121.1 10.9 %slice-start.2 = ((s8[5242880]{0:T(1024)(128)(4,1)}), s8[4194304]{0:T(1024)(128)(4,1)S(1)}, s32[]{:S(2)}) async-start(s8[5242880]{0:T(1024)(128)(4,1)} %bitcast.48), calls=%async_computation.6 | async-start | bytes 8388608
  127.1 3.8 %slice-start.1 = ((s8[5242880]{0:T(1024)(128)(4,1)}), s8[1048576]{0:T(1024)(128)(4,1)S(1)}, s32[]{:S(2)}) async-start(s8[5242880]{0:T(1024)(128)(4,1)} %bitcast.46), calls=%async_computation.5 | async-start | bytes 2097152
  128.0 3.9 %slice-start.3 = ((s8[5242880]{0:T(1024)(128)(4,1)}), s8[1048576]{0:T(1024)(128)(4,1)S(1)}, s32[]{:S(2)}) async-start(s8[5242880]{0:T(1024)(128)(4,1)} %bitcast.48), calls=%async_computation.7 | async-start | bytes 2097152
  133.0 29.1 %copy-start.1 = (bf16[4,5120]{1,0:T(4,128)(2,1)S(1)}, bf16[4,5120]{1,0:T(4,128)(2,1)}, u32[]{:S(2)}) copy-start(bf16[4,5120]{1,0:T(4,128)(2,1)} %param.11) | copy-start | bytes 122884
  158.0 49.0 %collective-permute-start = (f32[8,5120]{1,0:T(8,128)S(1)}, f32[8,5120]{1,0:T(8,128)S(1)}, u32[]{:S(2)}, u32[]{:S(2)}) collective-permute-start(f32[8,5120]{1,0:T(8,128)S(1)} %fusion), channel_id=1, source_target_pairs={{0,2},{2,4},{4,6},{6,8},{8,10},{10,12},{12,14},{1,3},{3,5},{5,7},{... | collective-permute-start | bytes 491528
  160.3 46.7 %collective-permute-start.1 = (f32[6,5120]{1,0:T(8,128)S(1)}, f32[6,5120]{1,0:T(8,128)S(1)}, u32[]{:S(2)}, u32[]{:S(2)}) collective-permute-start(f32[6,5120]{1,0:T(8,128)S(1)} %slice.34), channel_id=1, source_target_pairs={{0,4},{2,6},{4,8},{6,10},{8,12},{10,14},{1,5},{3,7},{5,9},{7,11},{... | collective-permute-start | bytes 368648
  200.4 4.7 %copy-start.2 = (bf16[4]{0:T(256)(128)(2,1)S(1)}, bf16[4]{0:T(256)(128)(2,1)}, u32[]{:S(2)}) copy-start(bf16[4]{0:T(256)(128)(2,1)} %param.14) | copy-start | bytes 28
  200.5 4.7 %copy-start.3 = (u32[32]{0:T(128)S(1)}, u32[32]{0:T(128)}, u32[]{:S(2)}) copy-start(u32[32]{0:T(128)} %constant.99) | copy-start | bytes 388
Sparse Core Ops, SparseCore 0:
  205.2 90.8 all-reduce.7
where the time goes:
time: 305 us
  blocking collectives  123 us (40%)
  waiting for transfers between devices  83.9 us (28%)
  local copies, waits for them, and re-layouts  43.5 us (14%)
  matrix products  22 us (7%)
  between operations  16.2 us (5%)
  starting transfers between devices  10.6 us (3%)
  other arithmetic  5.29 us (2%)
    unnamed x4, waiting for transfers between devices  83.9 us
    unnamed x4, blocking collectives  66.7 us
    unnamed x32, local copies, waits for them, and re-layouts  40.3 us
    all_gather x1, blocking collectives, body(): rows = lax.all_gather(arrived, 'expert', axis=0, tiled=True)  31.5 us
    all_gather x1, blocking collectives, shared_apart(): lax.all_gather(tokens, ('expert', 'narrow'), axis=0, tiled=True)  20.9 us
  transfers between devices with their start and end apart: 5, of which 1 were waited for; matrix products, arithmetic and copies ran while one was open for 10% of the time, Pallas kernels for 0%

commit v1 on v0

v1 whole, which is shorter than its diff:
```python
import functools

import jax
import jax.numpy as jnp
from jax import lax
from jax.experimental import pallas as pl
from jax.experimental.pallas import tpu as pltpu
from jax.sharding import PartitionSpec as P

META = 128
LANE = 128
STEP = 512
DOWN_CHUNK = 1280


def expert_swap(x, bits):
    size = lax.axis_size("expert")
    return lax.ppermute(x, "expert", [(i, i ^ bits) for i in range(size)])


def narrow_swap(x):
    return lax.ppermute(x, "narrow", [(0, 1), (1, 0)])


def token_index(row, tok_rows, outer, expert, narrow):
    block = row // tok_rows
    other_narrow = block // outer
    other_low = (block % outer) // (outer // 2)
    other_high = block % (outer // 2)
    from_expert = expert ^ (2 * other_high + other_low)
    from_narrow = narrow ^ other_narrow
    return (from_expert * 2 + from_narrow) * tok_rows + row % tok_rows


def layer_kernel(
    split_hot,
    tok_rows,
    outer,
    here_ref,
    far_ref,
    shared_in_ref,
    cold_in_ref,
    hot_in_ref,
    shared_out_ref,
    cold_out_ref,
    hot_out_ref,
    mine_ref,
    other_ref,
    x_ref,
    spread_ref,
    shared_in,
    cold_in,
    hot_in,
    shared_out,
    cold_out,
    hot_out,
    in_sems,
    out_sems,
):
    width = shared_in_ref.shape[0]
    narrow = lax.axis_index("narrow")
    expert = lax.axis_index("expert")
    half = here_ref.shape[0]
    rows = 2 * half
    hot_cols = hot_in.shape[0] * LANE

    copies = {}
    for which, (source, target) in enumerate(
        (
            (shared_in_ref, shared_in),
            (cold_in_ref.at[0], cold_in),
            (hot_in_ref, hot_in),
        )
    ):
        flat = source.reshape(2 * width, source.shape[2])
        base = narrow * hot_cols if (which == 2 and split_hot) else 0
        for tile in range(target.shape[0]):
            start = base + tile * LANE
            if not isinstance(start, int):
                start = pl.multiple_of(start, LANE)
            copies["in", which, tile] = pltpu.make_async_copy(
                flat.at[:, pl.ds(start, LANE)], target.at[tile], in_sems.at[which, tile]
            )
    chunks = width // DOWN_CHUNK
    for chunk in range(chunks):
        columns = pl.ds(chunk * DOWN_CHUNK, DOWN_CHUNK)
        for which, (source, target) in enumerate(
            ((shared_out_ref, shared_out), (cold_out_ref.at[0], cold_out), (hot_out_ref, hot_out))
        ):
            taken = source.at[:, columns]
            if which == 2 and split_hot:
                taken = source.at[pl.ds(pl.multiple_of(narrow * hot_cols, LANE), hot_cols), columns]
            copies["out", which, chunk] = pltpu.make_async_copy(
                taken, target.at[:, columns], out_sems.at[which, chunk]
            )
    for copy in copies.values():
        copy.start()

    x_ref[pl.ds(0, half)] = here_ref[...]
    x_ref[pl.ds(half, half)] = far_ref[...]

    meta = x_ref[:, pl.ds(width, META)].astype(jnp.float32)
    ids, plan, gate = meta[:, 0:1], meta[:, 1:2], meta[:, 2:3]
    hot = ids == 2.0
    dest = jnp.where(hot, plan, ids)
    index_of = functools.partial(
        token_index, tok_rows=tok_rows, outer=outer, expert=expert, narrow=narrow
    )
    column_index = index_of(lax.broadcasted_iota(jnp.int32, (rows, rows), 0))
    row_index = index_of(lax.broadcasted_iota(jnp.int32, (rows, rows), 1))
    before = (row_index < column_index).astype(jnp.float32).astype(jnp.bfloat16)
    lane = lax.broadcasted_iota(jnp.int32, (rows, META), 1).astype(jnp.float32)
    onehot = (lane == dest).astype(jnp.float32)
    counts = jnp.dot(before, onehot.astype(jnp.bfloat16), preferred_element_type=jnp.float32)
    rank = jnp.sum(onehot * counts, axis=1, keepdims=True)
    at_home = dest == narrow.astype(jnp.float32)
    limit = jnp.where(at_home, meta[0:1, 3:4], meta[half : half + 1, 3:4])
    kept = rank < limit
    cold_rows = kept & at_home & jnp.logical_not(hot)
    hot_rows = kept & hot
    if not split_hot:
        hot_rows = hot_rows & at_home

    source_lane = lax.broadcasted_iota(jnp.int32, (LANE, 4 * LANE), 0)
    target_lane = lax.broadcasted_iota(jnp.int32, (LANE, 4 * LANE), 1)
    aim = jnp.where(target_lane < 2 * LANE, 2 * source_lane, 2 * source_lane + 1 + 2 * LANE)
    spread = (target_lane == aim).astype(jnp.float32).astype(jnp.bfloat16)
    for block in range(width // LANE):
        wide = jnp.dot(
            x_ref[:, pl.ds(block * LANE, LANE)], spread, preferred_element_type=jnp.float32
        ).astype(jnp.bfloat16)
        columns = pl.ds(block * 2 * LANE, 2 * LANE)
        spread_ref[pl.ds(0, rows), columns] = wide[:, : 2 * LANE]
        spread_ref[pl.ds(rows, rows), columns] = wide[:, 2 * LANE :]

    def hidden(which, weights, keep):
        tiles = weights.shape[0]
        for tile in range(tiles):
            copies["in", which, tile].wait()
        parts = []
        group = 2 if tiles % 2 == 0 else 1
        for first in range(0, tiles, group):
            total = jnp.zeros((2 * rows, group * LANE), jnp.float32)
            for step in range(2 * width // (2 * STEP)):
                depth = pl.ds(step * 2 * STEP, 2 * STEP)
                block = weights[first, depth, :]
                if group == 2:
                    block = jnp.concatenate([block, weights[first + 1, depth, :]], axis=1)
                total = total + jnp.dot(
                    spread_ref[:, depth], block, preferred_element_type=jnp.float32
                )
            value = jax.nn.silu(total[:rows]) * total[rows:]
            if keep is not None:
                value = jnp.where(keep, value, 0.0)
            parts.append(value.astype(jnp.bfloat16))
        return parts[0] if len(parts) == 1 else jnp.concatenate(parts, axis=1)

    shared_hidden = hidden(0, shared_in, None)
    cold_hidden = hidden(1, cold_in, cold_rows)
    hot_hidden = hidden(2, hot_in, hot_rows)
    for chunk in range(chunks):
        columns = pl.ds(chunk * DOWN_CHUNK, DOWN_CHUNK)
        for which in range(3):
            copies["out", which, chunk].wait()
        routed = jnp.dot(cold_hidden, cold_out[:, columns], preferred_element_type=jnp.float32)
        routed = routed + jnp.dot(
            hot_hidden, hot_out[:, columns], preferred_element_type=jnp.float32
        )
        total = gate * routed + jnp.dot(
            shared_hidden, shared_out[:, columns], preferred_element_type=jnp.float32
        )
        mine_ref[:, columns] = total[:half]
        other_ref[:, columns] = total[half:].astype(jnp.bfloat16)


def layer(here, far, weights, tok_rows):
    shared_in, cold_in, hot_in, shared_out, cold_out, hot_out = weights
    outer = lax.axis_size("expert")
    width, _, part = shared_in.shape
    cold_part = cold_in.shape[3]
    hot_part = hot_in.shape[2]
    split_hot = hot_part % (2 * LANE) == 0
    hot_used = hot_part // 2 if split_hot else hot_part
    half = here.shape[0]
    kernel = functools.partial(layer_kernel, split_hot, tok_rows, outer)
    tiles = max(part, cold_part, hot_used) // LANE
    in_vmem = pl.BlockSpec(memory_space=pltpu.VMEM)
    anywhere = pl.BlockSpec(memory_space=pl.ANY)
    return pl.pallas_call(
        kernel,
        out_shape=(
            jax.ShapeDtypeStruct((half, width), jnp.float32),
            jax.ShapeDtypeStruct((half, width), jnp.bfloat16),
        ),
        in_specs=[in_vmem, in_vmem] + [anywhere] * 6,
        out_specs=(in_vmem, in_vmem),
        scratch_shapes=[
            pltpu.VMEM((2 * half, width + META), jnp.bfloat16),
            pltpu.VMEM((4 * half, 2 * width), jnp.bfloat16),
            pltpu.VMEM((part // LANE, 2 * width, LANE), jnp.bfloat16),
            pltpu.VMEM((cold_part // LANE, 2 * width, LANE), jnp.bfloat16),
            pltpu.VMEM((hot_used // LANE, 2 * width, LANE), jnp.bfloat16),
            pltpu.VMEM((part, width), jnp.bfloat16),
            pltpu.VMEM((cold_part, width), jnp.bfloat16),
            pltpu.VMEM((hot_used, width), jnp.bfloat16),
            pltpu.SemaphoreType.DMA((3, tiles)),
            pltpu.SemaphoreType.DMA((3, width // DOWN_CHUNK)),
        ],
        compiler_params=pltpu.CompilerParams(vmem_limit_bytes=56 << 20),
        name="layer",
    )(here, far, *weights)


def body(
    tokens,
    expert_ids,
    replica_plan,
    route_gate,
    capacity,
    cold_gate_up,
    cold_down,
    hot_gate_up,
    hot_down,
    shared_gate_up,
    shared_down,
):
    tok_rows, width = tokens.shape
    outer = lax.axis_size("expert")
    high = outer // 2
    lane = jnp.arange(META, dtype=jnp.int32)[None, :]
    meta = jnp.where(lane == 0, expert_ids.astype(jnp.bfloat16)[:, None], jnp.bfloat16(0))
    meta = jnp.where(lane == 1, replica_plan.astype(jnp.bfloat16)[:, None], meta)
    meta = jnp.where(lane == 2, route_gate[:, None], meta)
    meta = jnp.where(lane == 3, capacity.astype(jnp.bfloat16)[:, None], meta)
    packed = jnp.concatenate([tokens, meta], axis=1)
    line = jnp.concatenate(
        [packed] + [expert_swap(packed, 2 * step) for step in range(1, high)], axis=0
    )
    here = jnp.concatenate([line, expert_swap(line, 1)], axis=0)
    far = narrow_swap(here)
    weights = (shared_gate_up, cold_gate_up, hot_gate_up, shared_down, cold_down, hot_down)
    mine, other = layer(here, far, weights, tok_rows)
    mine = mine + narrow_swap(other).astype(jnp.float32)
    part = tok_rows * high
    mine = mine[:part] + expert_swap(mine[part:].astype(jnp.bfloat16), 1).astype(jnp.float32)
    total = mine[:tok_rows]
    for step in range(1, high):
        block = mine[step * tok_rows : (step + 1) * tok_rows].astype(jnp.bfloat16)
        total = total + expert_swap(block, 2 * step).astype(jnp.float32)
    return total.astype(jnp.bfloat16)


def solution(mesh):
    in_specs = (
        P(("groups", "expert", "narrow"), None),
        P(("groups", "expert", "narrow")),
        P(("groups", "expert", "narrow")),
        P(("groups", "expert", "narrow")),
        P(("groups", "narrow")),
        P("narrow", None, None, "expert"),
        P("narrow", "expert", None),
        P(None, None, "expert"),
        P("expert", None),
        P(None, None, ("expert", "narrow")),
        P(("expert", "narrow"), None),
    )
    out_specs = P(("groups", "expert", "narrow"), None)
    return jax.shard_map(body, mesh=mesh, in_specs=in_specs, out_specs=out_specs, check_vma=False)
```

time: 305 us -> 60.8 us (0.20)
  blocking collectives: 123 us -> 0 us
  waiting for transfers between devices: 83.9 us -> 21.1 us
  local copies, waits for them, and re-layouts: 43.5 us -> 1.03 us
  matrix products: 22 us -> 0 us
  Pallas kernels: 0 us -> 19.3 us
  between operations: 16.2 us -> 0.73 us
    unnamed x4 -> x0, waiting for transfers between devices: 83.9 us -> none
    unnamed x4 -> x0, blocking collectives: 66.7 us -> none
    all_gather x2 -> x0, blocking collectives: 52.4 us -> none  [the longest x1 31.5 us: body(): rows = lax.all_gather(arrived, 'expert', axis=0, tiled=True)]
    unnamed x32 -> x4, local copies, waits for them, and re-layouts: 40.3 us -> 0.75 us
    dot_general x9 -> x0, matrix products: 22 us -> none  [the longest x1 6.03 us: expert_partial(): jnp.dot(packed, cold_gate_up[0].reshape(width, 2 * part_width), preferred...]
    ppermute x0 -> x10, waiting for transfers between devices: none -> 21.1 us  [the longest x8 17.7 us: expert_swap(): return lax.ppermute(x, 'expert', [(i, i ^ bits) for i in range(size)])]
    pallas_call x0 -> x1, Pallas kernels: none -> 19.3 us  [layer(): pl.pallas_call(kernel, out_shape=(jax.ShapeDtypeStruct((half, width), jnp...]
    ppermute x0 -> x10, starting transfers between devices: none -> 12.7 us  [the longest x8 12.5 us: expert_swap(): return lax.ppermute(x, 'expert', [(i, i ^ bits) for i in range(size)])]
  transfers between devices with their start and end apart: 5 -> 10, of which waited for: 1 -> 9; matrix products, arithmetic and copies ran while one was open for 10% -> 0% of each run, Pallas kernels for 0% -> 0%
where the time goes in v1:
time: 60.8 us; the launch traced here: 60.5 us
  waiting for transfers between devices  21.1 us (35%)
  Pallas kernels  19.3 us (32%)
  starting transfers between devices  12.7 us (21%)
  other arithmetic  5.59 us (9%)
  local copies, waits for them, and re-layouts  1.03 us (2%)
  between operations  0.73 us (1%)
    pallas_call x1, Pallas kernels, layer(): pl.pallas_call(kernel, out_shape=(jax.ShapeDtypeStruct((half, width), jnp...  19.3 us
    ppermute x8, waiting for transfers between devices, expert_swap(): return lax.ppermute(x, 'expert', [(i, i ^ bits) for i in range(size)])  17.7 us
    ppermute x8, starting transfers between devices, expert_swap(): return lax.ppermute(x, 'expert', [(i, i ^ bits) for i in range(size)])  12.5 us
    ppermute x2, waiting for transfers between devices, narrow_swap(): return lax.ppermute(x, 'narrow', [(0, 1), (1, 0)])  3.34 us
  transfers between devices with their start and end apart: 10, of which 9 were waited for; matrix products, arithmetic and copies ran while one was open for 0% of the time, Pallas kernels for 0%

profile of v1, /device:TPU:0, one launch (start us, length us, event | category | flops | bytes accessed | tf_op | source)
XLA Modules:
  0.0 60.5 jit_solution(13470426914575314245)
XLA Ops:
  0.7 0.7 %convert_element_type.33 = bf16[4]{0:T(256)(128)(2,1)S(1)} convert(s32[4]{0:T(128)} %param.12) | non-fusion elementwise | flops 4 | bytes 24 | tf_op jit(solution)/shard_map/convert_element_type | solution.py:231
  1.3 0.7 %convert_element_type.32 = bf16[4]{0:T(256)(128)(2,1)S(1)} convert(s32[4]{0:T(128)} %param.13) | non-fusion elementwise | flops 4 | bytes 24 | tf_op jit(solution)/shard_map/convert_element_type | solution.py:232
  2.0 0.7 %select_select_fusion = bf16[4,128]{1,0:T(4,128)(2,1)S(1)} fusion(pred[128]{0:T(512)(128)(4,1)S(1)} %get-tuple-element.14, pred[128]{0:T(512)(128)(4,1)S(1)} %get-tuple-element.15, pred[128]{0:T(512)(128)(4,1)S(1)} %get-tuple-element.16, pred[128]{0:T(512)(128)(4,1)S(1)} %get-tuple-element.17, bf16[4]{0:T(256)(128)(2,1)S(1)} %convert_element_type.32, ...), kind=kLoop, calls=%fused_computation.9 | loop fusion | flops 2048 | bytes 1562 | tf_op jit(solution)/shard_map/jit(_where)/select_n | solution.py:234
  2.7 0.8 %pad_maximum_fusion.1 = bf16[4,5248]{1,0:T(4,128)(2,1)S(1)} fusion(bf16[4,128]{1,0:T(4,128)(2,1)S(1)} %select_select_fusion, bf16[4,5120]{1,0:T(4,128)(2,1)} %param.11), kind=kLoop, calls=%fused_computation.8 | loop fusion | flops 83968 | bytes 83968 | tf_op jit(solution)/shard_map/concatenate | solution.py:235
  3.5 5.1 %collective-permute-start.2 = (bf16[4,5248]{1,0:T(4,128)(2,1)S(1)}, bf16[4,5248]{1,0:T(4,128)(2,1)S(1)}, u32[]{:S(2)}, u32[]{:S(2)}) collective-permute-start(bf16[4,5248]{1,0:T(4,128)(2,1)S(1)} %pad_maximum_fusion.1), channel_id=1, source_target_pairs={{0,12},{2,14},{4,8},{6,10},{8,4},{10,6},{12,0},{14,2},{1,13},{3,15... | collective-permute-start | bytes 125960 | tf_op jit(solution)/shard_map/ppermute | solution.py:18
  8.6 0.0 collective-permute-start.1
  8.6 0.6 %collective-permute-start = (bf16[4,5248]{1,0:T(4,128)(2,1)S(1)}, bf16[4,5248]{1,0:T(4,128)(2,1)S(1)}, u32[]{:S(2)}, u32[]{:S(2)}) collective-permute-start(bf16[4,5248]{1,0:T(4,128)(2,1)S(1)} %pad_maximum_fusion.1), channel_id=1, source_target_pairs={{0,4},{2,6},{4,0},{6,2},{8,12},{10,14},{12,8},{14,10},{1,5},{3,7},... | collective-permute-start | bytes 125960 | tf_op jit(solution)/shard_map/ppermute | solution.py:18
  9.3 1.4 %collective-permute-done.2 = bf16[4,5248]{1,0:T(4,128)(2,1)S(1)} collective-permute-done((bf16[4,5248]{1,0:T(4,128)(2,1)S(1)}, bf16[4,5248]{1,0:T(4,128)(2,1)S(1)}, u32[]{:S(2)}, u32[]{:S(2)}) %collective-permute-start.2) | collective-permute-done | bytes 42016 | tf_op jit(solution)/shard_map/ppermute | solution.py:18
  10.7 2.9 %collective-permute-done.1 = bf16[4,5248]{1,0:T(4,128)(2,1)S(1)} collective-permute-done((bf16[4,5248]{1,0:T(4,128)(2,1)S(1)}, bf16[4,5248]{1,0:T(4,128)(2,1)S(1)}, u32[]{:S(2)}, u32[]{:S(2)}) %collective-permute-start.1) | collective-permute-done | bytes 42016 | tf_op jit(solution)/shard_map/ppermute | solution.py:18
  13.5 0.0 collective-permute-done
  13.6 0.9 %pad_maximum_fusion = bf16[16,5248]{1,0:T(8,128)(2,1)S(1)} fusion(bf16[4,5248]{1,0:T(4,128)(2,1)S(1)} %collective-permute-done.2, bf16[4,5248]{1,0:T(4,128)(2,1)S(1)} %collective-permute-done.1, bf16[4,5248]{1,0:T(4,128)(2,1)S(1)} %collective-permute-done, bf16[4,128]{1,0:T(4,128)(2,1)S(1)} %select_select_fusion, bf16[4,5120]{1,0:T(4,128)(2,1)} %param.11), kind=kLoop, calls=%fused_computation.3 | loop fusion | flops 839680 | bytes 335872 | tf_op jit(solution)/shard_map/concatenate | solution.py:236
  14.4 1.6 %collective-permute-start.3 = (bf16[16,5248]{1,0:T(8,128)(2,1)S(1)}, bf16[16,5248]{1,0:T(8,128)(2,1)S(1)}, u32[]{:S(2)}, u32[]{:S(2)}) collective-permute-start(bf16[16,5248]{1,0:T(8,128)(2,1)S(1)} %pad_maximum_fusion), channel_id=1, source_target_pairs={{0,2},{2,0},{4,6},{6,4},{8,10},{10,8},{12,14},{14,12},{1,3},{3,1},... | collective-permute-start | bytes 503816 | tf_op jit(solution)/shard_map/ppermute | solution.py:18
  16.0 3.8 %collective-permute-done.3 = bf16[16,5248]{1,0:T(8,128)(2,1)S(1)} collective-permute-done((bf16[16,5248]{1,0:T(8,128)(2,1)S(1)}, bf16[16,5248]{1,0:T(8,128)(2,1)S(1)}, u32[]{:S(2)}, u32[]{:S(2)}) %collective-permute-start.3) | collective-permute-done | bytes 167968 | tf_op jit(solution)/shard_map/ppermute | solution.py:18
  19.9 0.2 concatenate.12.here_ref
  20.1 0.0 copy-start
  20.1 0.1 collective-permute-start.4
  20.2 1.6 %collective-permute-done.4.far_ref = bf16[32,5248]{1,0:T(8,128)(2,1)S(1)} collective-permute-done((bf16[32,5248]{1,0:T(8,128)(2,1)S(1)}, bf16[32,5248]{1,0:T(8,128)(2,1)S(1)}, u32[]{:S(2)}, u32[]{:S(2)}) %collective-permute-start.4) | collective-permute-done | bytes 335904 | tf_op jit(solution)/shard_map/ppermute | solution.py:22
  21.8 0.0 copy-done
  21.8 0.0 copy-start.1
  21.8 0.7 %copy-done.1 = bf16[32,5248]{1,0:T(8,128)(2,1)} copy-done((bf16[32,5248]{1,0:T(8,128)(2,1)}, bf16[32,5248]{1,0:T(8,128)(2,1)S(1)}, u32[]{:S(2)}) %copy-start.1) | copy-done | bytes 335896
  22.5 19.3 %layer.1 = (f32[32,5120]{1,0:T(8,128)}, bf16[32,5120]{1,0:T(8,128)(2,1)}) custom-call(bf16[32,5248]{1,0:T(8,128)(2,1)} %copy-done, bf16[32,5248]{1,0:T(8,128)(2,1)} %copy-done.1, bf16[5120,2,512]{2,1,0:T(2,128)(2,1)} %shared_in_ref.1, bf16[1,5120,2,512]{3,2,1,0:T(2,128)(2,1)} %cold_in_ref.1, bf16[5120,2,512]{2,1,0:T(2,128)(2,1)} %hot_in_ref.1, ...), custom_call_target="tpu_custom_call" | custom-call | tf_op jit(solution)/shard_map/layer/pallas_call | solution.py:189
  41.9 0.2 collective-permute-start.5
  42.1 1.7 %collective-permute-done.5 = bf16[32,5120]{1,0:T(8,128)(2,1)S(1)} collective-permute-done((bf16[32,5120]{1,0:T(8,128)(2,1)}, bf16[32,5120]{1,0:T(8,128)(2,1)S(1)}, u32[]{:S(2)}, u32[]{:S(2)}) %collective-permute-start.5) | collective-permute-done | bytes 327712 | tf_op jit(solution)/shard_map/ppermute | solution.py:22
  43.8 1.1 %convert_add_fusion = f32[32,5120]{1,0:T(8,128)S(1)} fusion(f32[32,5120]{1,0:T(8,128)} %get-tuple-element.7, bf16[32,5120]{1,0:T(8,128)(2,1)S(1)} %collective-permute-done.5), kind=kLoop, calls=%fused_computation | loop fusion | flops 327680 | bytes 1638400 | tf_op jit(solution)/shard_map/add | solution.py:243
  45.0 1.6 %collective-permute-start.6 = (bf16[16,5120]{1,0:T(8,128)(2,1)S(1)}, bf16[16,5120]{1,0:T(8,128)(2,1)S(1)}, u32[]{:S(2)}, u32[]{:S(2)}) collective-permute-start(bf16[16,5120]{1,0:T(8,128)(2,1)S(1)} %slice.43), channel_id=1, source_target_pairs={{0,2},{2,0},{4,6},{6,4},{8,10},{10,8},{12,14},{14,12},{1,3},{3,1},... | collective-permute-start | bytes 491528 | tf_op jit(solution)/shard_map/ppermute | solution.py:18
  46.5 4.7 %collective-permute-done.6 = bf16[16,5120]{1,0:T(8,128)(2,1)S(1)} collective-permute-done((bf16[16,5120]{1,0:T(8,128)(2,1)S(1)}, bf16[16,5120]{1,0:T(8,128)(2,1)S(1)}, u32[]{:S(2)}, u32[]{:S(2)}) %collective-permute-start.6) | collective-permute-done | bytes 163872 | tf_op jit(solution)/shard_map/ppermute | solution.py:18
  51.3 0.1 fusion.4
  51.4 0.3 collective-permute-start.7
  51.6 3.3 %collective-permute-start.9 = (bf16[4,5120]{1,0:T(4,128)(2,1)S(1)}, bf16[4,5120]{1,0:T(4,128)(2,1)S(1)}, u32[]{:S(2)}, u32[]{:S(2)}) collective-permute-start(bf16[4,5120]{1,0:T(4,128)(2,1)S(1)} %get-tuple-element.12), channel_id=1, source_target_pairs={{0,12},{2,14},{4,8},{6,10},{8,4},{10,6},{12,0},{14,2},{1,13},{3,15... | collective-permute-start | bytes 122888 | tf_op jit(solution)/shard_map/ppermute | solution.py:18
  54.9 0.0 collective-permute-start.8
  54.9 1.0 %collective-permute-done.7 = bf16[4,5120]{1,0:T(4,128)(2,1)S(1)} collective-permute-done((bf16[4,5120]{1,0:T(4,128)(2,1)S(1)}, bf16[4,5120]{1,0:T(4,128)(2,1)S(1)}, u32[]{:S(2)}, u32[]{:S(2)}) %collective-permute-start.7) | collective-permute-done | bytes 40992 | tf_op jit(solution)/shard_map/ppermute | solution.py:18
  55.9 1.6 %collective-permute-done.9 = bf16[4,5120]{1,0:T(4,128)(2,1)S(1)} collective-permute-done((bf16[4,5120]{1,0:T(4,128)(2,1)S(1)}, bf16[4,5120]{1,0:T(4,128)(2,1)S(1)}, u32[]{:S(2)}, u32[]{:S(2)}) %collective-permute-start.9) | collective-permute-done | bytes 40992 | tf_op jit(solution)/shard_map/ppermute | solution.py:18
  57.5 2.3 %collective-permute-done.8 = bf16[4,5120]{1,0:T(4,128)(2,1)S(1)} collective-permute-done((bf16[4,5120]{1,0:T(4,128)(2,1)S(1)}, bf16[4,5120]{1,0:T(4,128)(2,1)S(1)}, u32[]{:S(2)}, u32[]{:S(2)}) %collective-permute-start.8) | collective-permute-done | bytes 40992 | tf_op jit(solution)/shard_map/ppermute | solution.py:18
  59.8 0.7 %fusion.2 = bf16[4,5120]{1,0:T(4,128)(2,1)} fusion(f32[16,5120]{1,0:T(8,128)S(1)} %get-tuple-element.10, bf16[4,5120]{1,0:T(4,128)(2,1)S(1)} %collective-permute-done.9, bf16[4,5120]{1,0:T(4,128)(2,1)S(1)} %collective-permute-done.8, bf16[4,5120]{1,0:T(4,128)(2,1)S(1)} %collective-permute-done.7), kind=kLoop, calls=%fused_computation.7 | loop fusion | flops 143360 | bytes 245760 | tf_op jit(solution)/shard_map/convert_element_type | solution.py:250
  (4 shorter events, 0.1 us)
Async XLA Ops:
  3.5 7.2 %collective-permute-start.2 = (bf16[4,5248]{1,0:T(4,128)(2,1)S(1)}, bf16[4,5248]{1,0:T(4,128)(2,1)S(1)}, u32[]{:S(2)}, u32[]{:S(2)}) collective-permute-start(bf16[4,5248]{1,0:T(4,128)(2,1)S(1)} %pad_maximum_fusion.1), channel_id=1, source_target_pairs={{0,12},{2,14},{4,8},{6,10},{8,4},{10,6},{12,0},{14,2},{1,13},{3,15... | collective-permute-start | bytes 125960 | tf_op jit(solution)/shard_map/ppermute | solution.py:18
  8.6 4.9 %collective-permute-start.1 = (bf16[4,5248]{1,0:T(4,128)(2,1)S(1)}, bf16[4,5248]{1,0:T(4,128)(2,1)S(1)}, u32[]{:S(2)}, u32[]{:S(2)}) collective-permute-start(bf16[4,5248]{1,0:T(4,128)(2,1)S(1)} %pad_maximum_fusion.1), channel_id=1, source_target_pairs={{0,8},{2,10},{4,12},{6,14},{8,0},{10,2},{12,4},{14,6},{1,9},{3,11}... | collective-permute-start | bytes 125960 | tf_op jit(solution)/shard_map/ppermute | solution.py:18
  8.6 4.9 %collective-permute-start = (bf16[4,5248]{1,0:T(4,128)(2,1)S(1)}, bf16[4,5248]{1,0:T(4,128)(2,1)S(1)}, u32[]{:S(2)}, u32[]{:S(2)}) collective-permute-start(bf16[4,5248]{1,0:T(4,128)(2,1)S(1)} %pad_maximum_fusion.1), channel_id=1, source_target_pairs={{0,4},{2,6},{4,0},{6,2},{8,12},{10,14},{12,8},{14,10},{1,5},{3,7},... | collective-permute-start | bytes 125960 | tf_op jit(solution)/shard_map/ppermute | solution.py:18
  14.4 5.4 %collective-permute-start.3 = (bf16[16,5248]{1,0:T(8,128)(2,1)S(1)}, bf16[16,5248]{1,0:T(8,128)(2,1)S(1)}, u32[]{:S(2)}, u32[]{:S(2)}) collective-permute-start(bf16[16,5248]{1,0:T(8,128)(2,1)S(1)} %pad_maximum_fusion), channel_id=1, source_target_pairs={{0,2},{2,0},{4,6},{6,4},{8,10},{10,8},{12,14},{14,12},{1,3},{3,1},... | collective-permute-start | bytes 503816 | tf_op jit(solution)/shard_map/ppermute | solution.py:18
  20.1 1.7 %copy-start = (bf16[32,5248]{1,0:T(8,128)(2,1)}, bf16[32,5248]{1,0:T(8,128)(2,1)S(1)}, u32[]{:S(2)}) copy-start(bf16[32,5248]{1,0:T(8,128)(2,1)S(1)} %concatenate.12.here_ref) | copy-start | bytes 1007620
  20.1 1.7 %collective-permute-start.4 = (bf16[32,5248]{1,0:T(8,128)(2,1)S(1)}, bf16[32,5248]{1,0:T(8,128)(2,1)S(1)}, u32[]{:S(2)}, u32[]{:S(2)}) collective-permute-start(bf16[32,5248]{1,0:T(8,128)(2,1)S(1)} %concatenate.12.here_ref), channel_id=1, source_target_pairs={{0,1},{1,0},{2,3},{3,2},{4,5},{5,4},{6,7},{7,6},{8,9},{9,8},{10,11... | collective-permute-start | bytes 1007624 | tf_op jit(solution)/shard_map/ppermute | solution.py:22
  21.8 0.7 %copy-start.1 = (bf16[32,5248]{1,0:T(8,128)(2,1)}, bf16[32,5248]{1,0:T(8,128)(2,1)S(1)}, u32[]{:S(2)}) copy-start(bf16[32,5248]{1,0:T(8,128)(2,1)S(1)} %collective-permute-done.4.far_ref) | copy-start | bytes 1007620
  41.9 1.9 %collective-permute-start.5 = (bf16[32,5120]{1,0:T(8,128)(2,1)}, bf16[32,5120]{1,0:T(8,128)(2,1)S(1)}, u32[]{:S(2)}, u32[]{:S(2)}) collective-permute-start(bf16[32,5120]{1,0:T(8,128)(2,1)} %get-tuple-element.8), channel_id=1, source_target_pairs={{0,1},{1,0},{2,3},{3,2},{4,5},{5,4},{6,7},{7,6},{8,9},{9,8},{10,11... | collective-permute-start | bytes 983048 | tf_op jit(solution)/shard_map/ppermute | solution.py:22
  45.0 6.3 %collective-permute-start.6 = (bf16[16,5120]{1,0:T(8,128)(2,1)S(1)}, bf16[16,5120]{1,0:T(8,128)(2,1)S(1)}, u32[]{:S(2)}, u32[]{:S(2)}) collective-permute-start(bf16[16,5120]{1,0:T(8,128)(2,1)S(1)} %slice.43), channel_id=1, source_target_pairs={{0,2},{2,0},{4,6},{6,4},{8,10},{10,8},{12,14},{14,12},{1,3},{3,1},... | collective-permute-start | bytes 491528 | tf_op jit(solution)/shard_map/ppermute | solution.py:18
  51.4 4.5 %collective-permute-start.7 = (bf16[4,5120]{1,0:T(4,128)(2,1)S(1)}, bf16[4,5120]{1,0:T(4,128)(2,1)S(1)}, u32[]{:S(2)}, u32[]{:S(2)}) collective-permute-start(bf16[4,5120]{1,0:T(4,128)(2,1)S(1)} %get-tuple-element.11), channel_id=1, source_target_pairs={{0,4},{2,6},{4,0},{6,2},{8,12},{10,14},{12,8},{14,10},{1,5},{3,7},... | collective-permute-start | bytes 122888 | tf_op jit(solution)/shard_map/ppermute | solution.py:18
  51.6 5.8 %collective-permute-start.9 = (bf16[4,5120]{1,0:T(4,128)(2,1)S(1)}, bf16[4,5120]{1,0:T(4,128)(2,1)S(1)}, u32[]{:S(2)}, u32[]{:S(2)}) collective-permute-start(bf16[4,5120]{1,0:T(4,128)(2,1)S(1)} %get-tuple-element.12), channel_id=1, source_target_pairs={{0,12},{2,14},{4,8},{6,10},{8,4},{10,6},{12,0},{14,2},{1,13},{3,15... | collective-permute-start | bytes 122888 | tf_op jit(solution)/shard_map/ppermute | solution.py:18
  54.9 4.9 %collective-permute-start.8 = (bf16[4,5120]{1,0:T(4,128)(2,1)S(1)}, bf16[4,5120]{1,0:T(4,128)(2,1)S(1)}, u32[]{:S(2)}, u32[]{:S(2)}) collective-permute-start(bf16[4,5120]{1,0:T(4,128)(2,1)S(1)} %get-tuple-element.13), channel_id=1, source_target_pairs={{0,8},{2,10},{4,12},{6,14},{8,0},{10,2},{12,4},{14,6},{1,9},{3,11}... | collective-permute-start | bytes 122888 | tf_op jit(solution)/shard_map/ppermute | solution.py:18

commit v2 on v1

v2 whole, which is shorter than its diff:
```python
import functools

import jax
import jax.numpy as jnp
from jax import lax
from jax.experimental import pallas as pl
from jax.experimental.pallas import tpu as pltpu
from jax.sharding import PartitionSpec as P

META = 128
LANE = 128
STEP = 512
DOWN_CHUNK = 2560


def expert_swap(x, bits):
    size = lax.axis_size("expert")
    return lax.ppermute(x, "expert", [(i, i ^ bits) for i in range(size)])


def narrow_swap(x):
    return lax.ppermute(x, "narrow", [(0, 1), (1, 0)])


def token_index(row, tok_rows, outer, expert, narrow):
    block = row // tok_rows
    other_narrow = block // outer
    other_low = (block % outer) // (outer // 2)
    other_high = block % (outer // 2)
    from_expert = expert ^ (2 * other_high + other_low)
    from_narrow = narrow ^ other_narrow
    return (from_expert * 2 + from_narrow) * tok_rows + row % tok_rows


def pack_kernel(tokens_ref, ids_ref, plan_ref, gate_ref, capacity_ref, packed_ref):
    rows, width = tokens_ref.shape
    packed_ref[:, pl.ds(0, width)] = tokens_ref[...]
    own = lax.broadcasted_iota(jnp.int32, (rows, rows), 0) == lax.broadcasted_iota(
        jnp.int32, (rows, rows), 1
    )

    def per_row(ref):
        spread = jnp.broadcast_to(ref[...].astype(jnp.float32), (rows, rows))
        return jnp.sum(jnp.where(own, spread, 0.0), axis=1, keepdims=True)

    lane = lax.broadcasted_iota(jnp.int32, (rows, META), 1)
    meta = jnp.where(lane == 0, per_row(ids_ref), 0.0)
    meta = jnp.where(lane == 1, per_row(plan_ref), meta)
    meta = jnp.where(lane == 2, per_row(gate_ref), meta)
    meta = jnp.where(lane == 3, capacity_ref[...].astype(jnp.float32), meta)
    packed_ref[:, pl.ds(width, META)] = meta.astype(jnp.bfloat16)


def pack(tokens, ids, plan, gate, capacity):
    rows, width = tokens.shape
    return pl.pallas_call(
        pack_kernel,
        out_shape=pltpu.VMEM((rows, width + META), jnp.bfloat16),
        in_specs=[pl.BlockSpec(memory_space=pltpu.VMEM)] * 5,
        out_specs=pl.BlockSpec(memory_space=pltpu.VMEM),
        name="pack",
    )(tokens, *(v.reshape(1, -1) for v in (ids, plan, gate, capacity)))


def tile_copies(source, target, sems, base):
    width = source.shape[0]
    flat = source.reshape(2 * width, source.shape[2])
    copies = []
    for tile in range(target.shape[0]):
        start = base + tile * LANE
        if not isinstance(start, int):
            start = pl.multiple_of(start, LANE)
        copies.append(
            pltpu.make_async_copy(
                flat.at[:, pl.ds(start, LANE)], target.at[tile], sems.at[tile]
            )
        )
    return copies


def spread_rows(x_ref, spread_ref, width):
    rows = x_ref.shape[0]
    source_lane = lax.broadcasted_iota(jnp.int32, (LANE, 4 * LANE), 0)
    target_lane = lax.broadcasted_iota(jnp.int32, (LANE, 4 * LANE), 1)
    aim = jnp.where(target_lane < 2 * LANE, 2 * source_lane, 2 * source_lane + 1 + 2 * LANE)
    spread = (target_lane == aim).astype(jnp.float32).astype(jnp.bfloat16)
    for block in range(width // LANE):
        wide = jnp.dot(
            x_ref[:, pl.ds(block * LANE, LANE)], spread, preferred_element_type=jnp.float32
        ).astype(jnp.bfloat16)
        columns = pl.ds(block * 2 * LANE, 2 * LANE)
        spread_ref[pl.ds(0, rows), columns] = wide[:, : 2 * LANE]
        spread_ref[pl.ds(rows, rows), columns] = wide[:, 2 * LANE :]


def fetch_kernel(source_ref, after_ref, target_ref, done_ref, sems):
    del after_ref
    source = source_ref if len(source_ref.shape) == 3 else source_ref.at[0]
    copies = tile_copies(source, target_ref, sems, 0)
    for copy in copies:
        copy.start()
    for copy in copies:
        copy.wait()
    done_ref[...] = jnp.zeros_like(done_ref)


def join_kernel(*refs):
    pieces, joined_ref = refs[1:-1], refs[-1]
    joined_ref[...] = jnp.concatenate(
        [piece[...].astype(jnp.float32) for piece in pieces], axis=0
    ).astype(joined_ref.dtype)


def join(after, pieces):
    rows, width = pieces[0].shape
    in_vmem = pl.BlockSpec(memory_space=pltpu.VMEM)
    return pl.pallas_call(
        join_kernel,
        out_shape=pltpu.VMEM((len(pieces) * rows, width), pieces[0].dtype),
        in_specs=[in_vmem] * (1 + len(pieces)),
        out_specs=in_vmem,
        compiler_params=pltpu.CompilerParams(vmem_limit_bytes=4 << 20),
        name="join",
    )(after, *pieces)


def fetch(source, after):
    width, _, part = source.shape[-3:]
    size = source.size * source.dtype.itemsize
    return pl.pallas_call(
        fetch_kernel,
        out_shape=(
            pltpu.VMEM((part // LANE, 2 * width, LANE), jnp.bfloat16),
            pltpu.VMEM((8, LANE), jnp.float32),
        ),
        in_specs=[pl.BlockSpec(memory_space=pltpu.HBM), pl.BlockSpec(memory_space=pltpu.VMEM)],
        out_specs=(pl.BlockSpec(memory_space=pltpu.VMEM),) * 2,
        scratch_shapes=[pltpu.SemaphoreType.DMA((part // LANE,))],
        cost_estimate=pl.CostEstimate(flops=0, bytes_accessed=2 * size, transcendentals=0),
        compiler_params=pltpu.CompilerParams(vmem_limit_bytes=4 << 20),
        name="fetch",
    )(pltpu.with_memory_space_constraint(source, pltpu.HBM), after)


def near_spread_kernel(here_ref, spread_ref):
    spread_rows(here_ref, spread_ref, spread_ref.shape[1] // 2)


def spread_near(here):
    half, width = here.shape[0], here.shape[1] - META
    in_vmem = pl.BlockSpec(memory_space=pltpu.VMEM)
    return pl.pallas_call(
        near_spread_kernel,
        out_shape=pltpu.VMEM((2 * half, 2 * width), jnp.bfloat16),
        in_specs=[in_vmem],
        out_specs=in_vmem,
        compiler_params=pltpu.CompilerParams(vmem_limit_bytes=4 << 20),
        name="spread",
    )(here)


def layer_kernel(
    split_hot,
    tok_rows,
    outer,
    here_ref,
    far_ref,
    near_spread_ref,
    shared_in,
    cold_in,
    hot_in_ref,
    shared_out,
    cold_out,
    hot_out_ref,
    mine_ref,
    other_ref,
    far_spread_ref,
    hot_in,
    hot_out,
    in_sems,
    out_sem,
    hid_ref,
):
    width = mine_ref.shape[1]
    narrow = lax.axis_index("narrow")
    expert = lax.axis_index("expert")
    half = here_ref.shape[0]
    rows = 2 * half
    hot_used = hot_out.shape[0]
    base = narrow * hot_used if split_hot else 0
    in_copies = tile_copies(hot_in_ref, hot_in, in_sems, base)
    taken = hot_out_ref
    if split_hot:
        taken = hot_out_ref.at[pl.ds(pl.multiple_of(base, LANE), hot_used)]
    out_copy = pltpu.make_async_copy(taken, hot_out, out_sem)
    for copy in (*in_copies, out_copy):
        copy.start()
    spread_rows(far_ref, far_spread_ref, width)

    meta = jnp.concatenate(
        [ref[:, pl.ds(width, META)].astype(jnp.float32) for ref in (here_ref, far_ref)], axis=0
    )
    ids, plan, gate = meta[:, 0:1], meta[:, 1:2], meta[:, 2:3]
    hot = ids == 2.0
    dest = jnp.where(hot, plan, ids)
    index_of = functools.partial(
        token_index, tok_rows=tok_rows, outer=outer, expert=expert, narrow=narrow
    )
    column_index = index_of(lax.broadcasted_iota(jnp.int32, (rows, rows), 0))
    row_index = index_of(lax.broadcasted_iota(jnp.int32, (rows, rows), 1))
    before = (row_index < column_index).astype(jnp.float32).astype(jnp.bfloat16)
    lane = lax.broadcasted_iota(jnp.int32, (rows, META), 1).astype(jnp.float32)
    onehot = (lane == dest).astype(jnp.float32)
    counts = jnp.dot(before, onehot.astype(jnp.bfloat16), preferred_element_type=jnp.float32)
    rank = jnp.sum(onehot * counts, axis=1, keepdims=True)
    at_home = dest == narrow.astype(jnp.float32)
    limit = jnp.where(at_home, meta[0:1, 3:4], meta[half : half + 1, 3:4])
    kept = rank < limit
    cold_rows = kept & at_home & jnp.logical_not(hot)
    hot_rows = kept & hot
    if not split_hot:
        hot_rows = hot_rows & at_home

    def hidden(weights, keep):
        tiles = weights.shape[0]
        group = hid_ref.shape[2] // LANE

        def pair(index, _):
            first = index * group
            total = jnp.zeros((2 * rows, group * LANE), jnp.float32)
            for step in range(2 * width // (2 * STEP)):
                depth = pl.ds(step * 2 * STEP, 2 * STEP)
                block = weights[first, depth, :]
                if group == 2:
                    block = jnp.concatenate([block, weights[first + 1, depth, :]], axis=1)
                spread = jnp.concatenate([near_spread_ref[:, depth], far_spread_ref[:, depth]], axis=0)
                total = total + jnp.dot(spread, block, preferred_element_type=jnp.float32)
            gate_in = jnp.concatenate([total[:half], total[rows : rows + half]], axis=0)
            up_in = jnp.concatenate([total[half:rows], total[rows + half :]], axis=0)
            value = jax.nn.silu(gate_in) * up_in
            if keep is not None:
                value = jnp.where(keep, value, 0.0)
            hid_ref[index] = value.astype(jnp.bfloat16)
            return 0

        lax.fori_loop(0, tiles // group, pair, 0)
        parts = [hid_ref[i] for i in range(tiles // group)]
        return parts[0] if len(parts) == 1 else jnp.concatenate(parts, axis=1)

    shared_hidden = hidden(shared_in, None)
    cold_hidden = hidden(cold_in, cold_rows)
    for copy in in_copies:
        copy.wait()
    hot_hidden = hidden(hot_in, hot_rows)
    out_copy.wait()
    def down(chunk, _):
        columns = pl.ds(pl.multiple_of(chunk * DOWN_CHUNK, DOWN_CHUNK), DOWN_CHUNK)
        routed = jnp.dot(cold_hidden, cold_out[:, columns], preferred_element_type=jnp.float32)
        routed = routed + jnp.dot(
            hot_hidden, hot_out[:, columns], preferred_element_type=jnp.float32
        )
        total = gate * routed + jnp.dot(
            shared_hidden, shared_out[:, columns], preferred_element_type=jnp.float32
        )
        mine_ref[:, columns] = total[:half]
        other_ref[:, columns] = total[half:].astype(jnp.bfloat16)
        return 0

    lax.fori_loop(0, width // DOWN_CHUNK, down, 0)


def layer(here, far, near_spread, weights, tok_rows):
    shared_in, cold_in, hot_in, shared_out, cold_out, hot_out = weights
    half = here.shape[0]
    width = here.shape[1] - META
    hot_part = hot_in.shape[2]
    split_hot = hot_part % (2 * LANE) == 0
    hot_used = hot_part // 2 if split_hot else hot_part
    in_vmem = pl.BlockSpec(memory_space=pltpu.VMEM)
    in_hbm = pl.BlockSpec(memory_space=pltpu.HBM)
    held = 8 * half * width + 6 * hot_used * width
    tiles = (shared_in.shape[0], cold_in.shape[0], hot_used // LANE)
    group = 2 if all(count % 2 == 0 for count in tiles) else 1
    most = max(tiles) // group
    return pl.pallas_call(
        functools.partial(layer_kernel, split_hot, tok_rows, lax.axis_size("expert")),
        out_shape=(
            pltpu.VMEM((half, width), jnp.float32),
            pltpu.VMEM((half, width), jnp.bfloat16),
        ),
        in_specs=[in_vmem] * 5 + [in_hbm] + [in_vmem] * 2 + [in_hbm],
        out_specs=(in_vmem, in_vmem),
        scratch_shapes=[
            pltpu.VMEM((2 * half, 2 * width), jnp.bfloat16),
            pltpu.VMEM((hot_used // LANE, 2 * width, LANE), jnp.bfloat16),
            pltpu.VMEM((hot_used, width), jnp.bfloat16),
            pltpu.SemaphoreType.DMA((hot_used // LANE,)),
            pltpu.SemaphoreType.DMA,
            pltpu.VMEM((most, 2 * half, LANE * group), jnp.bfloat16),
        ],
        compiler_params=pltpu.CompilerParams(vmem_limit_bytes=held + (4 << 20)),
        name="layer",
    )(
        here,
        far,
        pltpu.with_memory_space_constraint(near_spread, pltpu.VMEM),
        pltpu.with_memory_space_constraint(shared_in, pltpu.VMEM),
        pltpu.with_memory_space_constraint(cold_in, pltpu.VMEM),
        pltpu.with_memory_space_constraint(hot_in, pltpu.HBM),
        shared_out,
        cold_out,
        pltpu.with_memory_space_constraint(hot_out, pltpu.HBM),
    )


def body(
    tokens,
    expert_ids,
    replica_plan,
    route_gate,
    capacity,
    cold_gate_up,
    cold_down,
    hot_gate_up,
    hot_down,
    shared_gate_up,
    shared_down,
):
    tok_rows, width = tokens.shape
    outer = lax.axis_size("expert")
    high = outer // 2
    packed = pack(tokens, expert_ids, replica_plan, route_gate, capacity)
    shared_in, shared_held = fetch(shared_gate_up, packed)
    line = join(
        shared_held, [packed] + [expert_swap(packed, 2 * step) for step in range(1, high)]
    )
    cold_in, cold_held = fetch(cold_gate_up, line)
    here = join(cold_held, [line, expert_swap(line, 1)])
    near_spread = spread_near(here)
    far = narrow_swap(here)
    weights = (shared_in, cold_in, hot_gate_up, shared_down, cold_down[0], hot_down)
    mine, other = layer(here, far, near_spread, weights, tok_rows)
    mine = mine + narrow_swap(other).astype(jnp.float32)
    part = tok_rows * high
    mine = mine[:part] + expert_swap(mine[part:].astype(jnp.bfloat16), 1).astype(jnp.float32)
    total = mine[:tok_rows]
    for step in range(1, high):
        block = mine[step * tok_rows : (step + 1) * tok_rows].astype(jnp.bfloat16)
        total = total + expert_swap(block, 2 * step).astype(jnp.float32)
    return total.astype(jnp.bfloat16)


def solution(mesh):
    in_specs = (
        P(("groups", "expert", "narrow"), None),
        P(("groups", "expert", "narrow")),
        P(("groups", "expert", "narrow")),
        P(("groups", "expert", "narrow")),
        P(("groups", "narrow")),
        P("narrow", None, None, "expert"),
        P("narrow", "expert", None),
        P(None, None, "expert"),
        P("expert", None),
        P(None, None, ("expert", "narrow")),
        P(("expert", "narrow"), None),
    )
    out_specs = P(("groups", "expert", "narrow"), None)
    return jax.shard_map(body, mesh=mesh, in_specs=in_specs, out_specs=out_specs, check_vma=False)
```

time: 60.8 us -> 44.9 us (0.74)
  waiting for transfers between devices: 21.1 us -> 11.9 us
  other arithmetic: 5.59 us -> 0.76 us
  Pallas kernels: 19.3 us -> 18 us
  local copies, waits for them, and re-layouts: 1.03 us -> 0.11 us
    ppermute x8, waiting for transfers between devices: 17.7 us -> 9.57 us  [expert_swap(): return lax.ppermute(x, 'expert', [(i, i ^ bits) for i in range(size)])]
    concatenate x2 -> x0, other arithmetic: 1.68 us -> none  [the longest x1 0.88 us: body(): jnp.concatenate([packed] + [expert_swap(packed, 2 * step) for step in ran...]
    pallas_call x1 -> x7, Pallas kernels: 19.3 us -> 18 us  [the longest x2 8.19 us: fetch(): pl.pallas_call(fetch_kernel, out_shape=(pltpu.VMEM((part // LANE, 2 * wid...]
    convert_element_type x2 -> x0, other arithmetic: 1.32 us -> none  [the longest x1 0.66 us: body(): expert_ids.astype(jnp.bfloat16)[:, None]]
    add x1, other arithmetic: 1.14 us -> 0.06 us  [body(): mine = mine + narrow_swap(other).astype(jnp.float32)]
    ppermute x2, waiting for transfers between devices: 3.34 us -> 2.3 us  [narrow_swap(): return lax.ppermute(x, 'narrow', [(0, 1), (1, 0)])]
    select_n x1 -> x0, other arithmetic: 0.73 us -> none  [body(): meta = jnp.where(lane == 3, capacity.astype(jnp.bfloat16)[:, None], meta)]
    unnamed x4 -> x8, local copies, waits for them, and re-layouts: 0.75 us -> 0.04 us
  transfers between devices with their start and end apart: 10 -> 10, of which waited for: 9 -> 6; matrix products, arithmetic and copies ran while one was open for 0% -> 0% of each run, Pallas kernels for 0% -> 20%
where the time goes in v2:
time: 44.9 us; the launch traced here: 44.7 us
  Pallas kernels  18 us (40%)
  starting transfers between devices  13.2 us (29%)
  waiting for transfers between devices  11.9 us (27%)
  between operations  0.8 us (2%)
  other arithmetic  0.76 us (2%)
    ppermute x8, starting transfers between devices, expert_swap(): return lax.ppermute(x, 'expert', [(i, i ^ bits) for i in range(size)])  12.9 us
    ppermute x8, waiting for transfers between devices, expert_swap(): return lax.ppermute(x, 'expert', [(i, i ^ bits) for i in range(size)])  9.57 us
    pallas_call x2, Pallas kernels, fetch(): pl.pallas_call(fetch_kernel, out_shape=(pltpu.VMEM((part // LANE, 2 * wid...  8.19 us
    pallas_call x1, Pallas kernels, layer(): pl.pallas_call(functools.partial(layer_kernel, split_hot, tok_rows, lax.a...  8.02 us
    ppermute x2, waiting for transfers between devices, narrow_swap(): return lax.ppermute(x, 'narrow', [(0, 1), (1, 0)])  2.3 us
  transfers between devices with their start and end apart: 10, of which 6 were waited for; matrix products, arithmetic and copies ran while one was open for 0% of the time, Pallas kernels for 20%

profile of v2, /device:TPU:0, one launch (start us, length us, event | category | flops | bytes accessed | tf_op | source)
XLA Modules:
  0.0 44.7 jit_solution(6746736712236005917)
XLA Ops:
  0.7 0.9 %pack.1.after_ref.refs_1_ = bf16[4,5248]{1,0:T(4,128)(2,1)S(1)} custom-call(bf16[4,5120]{1,0:T(4,128)(2,1)} %tokens_ref.1, s32[1,4]{1,0:T(1,128)} %bitcast.11, s32[1,4]{1,0:T(1,128)} %bitcast.12, bf16[1,4]{1,0:T(2,128)(2,1)} %bitcast.13, s32[1,1]{1,0:T(1,128)} %bitcast.5.capacity_ref), custom_call_target="tpu_custom_call" | custom-call | tf_op jit(solution)/shard_map/pack/pallas_call | solution.py:56
  1.5 0.0 slice-start
  1.5 0.0 slice-start.2
  1.6 5.1 %collective-permute-start.2 = (bf16[4,5248]{1,0:T(4,128)(2,1)S(1)}, bf16[4,5248]{1,0:T(4,128)(2,1)S(1)}, u32[]{:S(2)}, u32[]{:S(2)}) collective-permute-start(bf16[4,5248]{1,0:T(4,128)(2,1)S(1)} %pack.1.after_ref.refs_1_), channel_id=1, source_target_pairs={{0,12},{2,14},{4,8},{6,10},{8,4},{10,6},{12,0},{14,2},{1,13},{3,15... | collective-permute-start | bytes 125960 | tf_op jit(solution)/shard_map/ppermute | solution.py:18
  6.7 0.0 collective-permute-start.1
  6.7 0.6 %collective-permute-start = (bf16[4,5248]{1,0:T(4,128)(2,1)S(1)}, bf16[4,5248]{1,0:T(4,128)(2,1)S(1)}, u32[]{:S(2)}, u32[]{:S(2)}) collective-permute-start(bf16[4,5248]{1,0:T(4,128)(2,1)S(1)} %pack.1.after_ref.refs_1_), channel_id=1, source_target_pairs={{0,4},{2,6},{4,0},{6,2},{8,12},{10,14},{12,8},{14,10},{1,5},{3,7},... | collective-permute-start | bytes 125960 | tf_op jit(solution)/shard_map/ppermute | solution.py:18
  7.3 4.1 %fetch.2 = (bf16[4,10240,128]{2,1,0:T(8,128)(2,1)S(1)}, f32[8,128]{1,0:T(8,128)S(1)}) custom-call(bf16[5120,2,512]{2,1,0:T(2,128)(2,1)} %source_ref.2, bf16[4,5248]{1,0:T(4,128)(2,1)S(1)} %pack.1.after_ref.refs_1_), custom_call_target="tpu_custom_call" | custom-call | bytes 20971520 | tf_op jit(solution)/shard_map/fetch/pallas_call | solution.py:130
  11.4 0.0 collective-permute-done.2.refs_4_
  11.4 0.2 collective-permute-done.1.refs_3_
  11.6 0.0 collective-permute-done.refs_2_
  11.6 0.0 slice-start.1
  11.6 0.0 slice-start.3
  11.7 1.6 %collective-permute-start.3 = (bf16[16,5248]{1,0:T(8,128)(2,1)S(1)}, bf16[16,5248]{1,0:T(8,128)(2,1)S(1)}, u32[]{:S(2)}, u32[]{:S(2)}) collective-permute-start(bf16[16,5248]{1,0:T(8,128)(2,1)S(1)} %join.2.after_ref.refs_1_), channel_id=1, source_target_pairs={{0,2},{2,0},{4,6},{6,4},{8,10},{10,8},{12,14},{14,12},{1,3},{3,1},... | collective-permute-start | bytes 503816 | tf_op jit(solution)/shard_map/ppermute | solution.py:18
  13.3 4.1 %fetch.3 = (bf16[4,10240,128]{2,1,0:T(8,128)(2,1)S(1)}, f32[8,128]{1,0:T(8,128)S(1)}) custom-call(bf16[1,5120,2,512]{3,2,1,0:T(2,128)(2,1)} %source_ref.3, bf16[16,5248]{1,0:T(8,128)(2,1)S(1)} %join.2.after_ref.refs_1_), custom_call_target="tpu_custom_call" | custom-call | bytes 20971520 | tf_op jit(solution)/shard_map/fetch/pallas_call | solution.py:130
  17.4 0.0 collective-permute-done.3.refs_2_
  17.4 0.1 collective-permute-start.4
  17.5 0.8 %spread.1.near_spread_ref = bf16[64,10240]{1,0:T(8,128)(2,1)S(1)} custom-call(bf16[32,5248]{1,0:T(8,128)(2,1)S(1)} %join.3.here_ref), custom_call_target="tpu_custom_call" | custom-call | tf_op jit(solution)/shard_map/spread/pallas_call | solution.py:152
  18.3 0.8 %collective-permute-done.4.far_ref = bf16[32,5248]{1,0:T(8,128)(2,1)S(1)} collective-permute-done((bf16[32,5248]{1,0:T(8,128)(2,1)S(1)}, bf16[32,5248]{1,0:T(8,128)(2,1)S(1)}, u32[]{:S(2)}, u32[]{:S(2)}) %collective-permute-start.4) | collective-permute-done | bytes 335904 | tf_op jit(solution)/shard_map/ppermute | solution.py:22
  19.1 0.0 slice-done
  19.1 0.0 slice-done.2
  19.1 0.0 slice-done.1
  19.1 0.0 slice-done.3
  19.1 8.0 %layer.1 = (f32[32,5120]{1,0:T(8,128)S(1)}, bf16[32,5120]{1,0:T(8,128)(2,1)S(1)}) custom-call(bf16[32,5248]{1,0:T(8,128)(2,1)S(1)} %join.3.here_ref, bf16[32,5248]{1,0:T(8,128)(2,1)S(1)} %collective-permute-done.4.far_ref, bf16[64,10240]{1,0:T(8,128)(2,1)S(1)} %spread.1.near_spread_ref, bf16[4,10240,128]{2,1,0:T(8,128)(2,1)S(1)} %get-tuple-element.13.shared_in, ...), custom_call_target="tpu_custom_call" | custom-call | tf_op jit(solution)/shard_map/layer/pallas_call | solution.py:285
  27.2 0.2 collective-permute-start.5
  27.4 1.5 %collective-permute-done.5 = bf16[32,5120]{1,0:T(8,128)(2,1)S(1)} collective-permute-done((bf16[32,5120]{1,0:T(8,128)(2,1)S(1)}, bf16[32,5120]{1,0:T(8,128)(2,1)S(1)}, u32[]{:S(2)}, u32[]{:S(2)}) %collective-permute-start.5) | collective-permute-done | bytes 327712 | tf_op jit(solution)/shard_map/ppermute | solution.py:22
  28.9 0.1 convert_add_fusion
  29.0 1.3 %collective-permute-start.6 = (bf16[16,5120]{1,0:T(8,128)(2,1)S(1)}, bf16[16,5120]{1,0:T(8,128)(2,1)S(1)}, u32[]{:S(2)}, u32[]{:S(2)}) collective-permute-start(bf16[16,5120]{1,0:T(8,128)(2,1)S(1)} %slice.43), channel_id=1, source_target_pairs={{0,2},{2,0},{4,6},{6,4},{8,10},{10,8},{12,14},{14,12},{1,3},{3,1},... | collective-permute-start | bytes 491528 | tf_op jit(solution)/shard_map/ppermute | solution.py:18
  30.3 5.0 %collective-permute-done.6 = bf16[16,5120]{1,0:T(8,128)(2,1)S(1)} collective-permute-done((bf16[16,5120]{1,0:T(8,128)(2,1)S(1)}, bf16[16,5120]{1,0:T(8,128)(2,1)S(1)}, u32[]{:S(2)}, u32[]{:S(2)}) %collective-permute-start.6) | collective-permute-done | bytes 163872 | tf_op jit(solution)/shard_map/ppermute | solution.py:18
  35.3 0.1 fusion.4
  35.4 1.3 %collective-permute-start.7 = (bf16[4,5120]{1,0:T(4,128)(2,1)S(1)}, bf16[4,5120]{1,0:T(4,128)(2,1)S(1)}, u32[]{:S(2)}, u32[]{:S(2)}) collective-permute-start(bf16[4,5120]{1,0:T(4,128)(2,1)S(1)} %get-tuple-element.19), channel_id=1, source_target_pairs={{0,4},{2,6},{4,0},{6,2},{8,12},{10,14},{12,8},{14,10},{1,5},{3,7},... | collective-permute-start | bytes 122888 | tf_op jit(solution)/shard_map/ppermute | solution.py:18
  36.7 2.4 %collective-permute-start.9 = (bf16[4,5120]{1,0:T(4,128)(2,1)S(1)}, bf16[4,5120]{1,0:T(4,128)(2,1)S(1)}, u32[]{:S(2)}, u32[]{:S(2)}) collective-permute-start(bf16[4,5120]{1,0:T(4,128)(2,1)S(1)} %get-tuple-element.20), channel_id=1, source_target_pairs={{0,12},{2,14},{4,8},{6,10},{8,4},{10,6},{12,0},{14,2},{1,13},{3,15... | collective-permute-start | bytes 122888 | tf_op jit(solution)/shard_map/ppermute | solution.py:18
  39.1 0.5 %collective-permute-start.8 = (bf16[4,5120]{1,0:T(4,128)(2,1)S(1)}, bf16[4,5120]{1,0:T(4,128)(2,1)S(1)}, u32[]{:S(2)}, u32[]{:S(2)}) collective-permute-start(bf16[4,5120]{1,0:T(4,128)(2,1)S(1)} %get-tuple-element.21), channel_id=1, source_target_pairs={{0,8},{2,10},{4,12},{6,14},{8,0},{10,2},{12,4},{14,6},{1,9},{3,11}... | collective-permute-start | bytes 122888 | tf_op jit(solution)/shard_map/ppermute | solution.py:18
  39.6 0.0 collective-permute-done.7
  39.6 3.2 %collective-permute-done.9 = bf16[4,5120]{1,0:T(4,128)(2,1)S(1)} collective-permute-done((bf16[4,5120]{1,0:T(4,128)(2,1)S(1)}, bf16[4,5120]{1,0:T(4,128)(2,1)S(1)}, u32[]{:S(2)}, u32[]{:S(2)}) %collective-permute-start.9) | collective-permute-done | bytes 40992 | tf_op jit(solution)/shard_map/ppermute | solution.py:18
  42.8 1.2 %collective-permute-done.8 = bf16[4,5120]{1,0:T(4,128)(2,1)S(1)} collective-permute-done((bf16[4,5120]{1,0:T(4,128)(2,1)S(1)}, bf16[4,5120]{1,0:T(4,128)(2,1)S(1)}, u32[]{:S(2)}, u32[]{:S(2)}) %collective-permute-start.8) | collective-permute-done | bytes 40992 | tf_op jit(solution)/shard_map/ppermute | solution.py:18
  44.0 0.7 %fusion.2 = bf16[4,5120]{1,0:T(4,128)(2,1)} fusion(f32[16,5120]{1,0:T(8,128)S(1)} %get-tuple-element.18, bf16[4,5120]{1,0:T(4,128)(2,1)S(1)} %collective-permute-done.9, bf16[4,5120]{1,0:T(4,128)(2,1)S(1)} %collective-permute-done.8, bf16[4,5120]{1,0:T(4,128)(2,1)S(1)} %collective-permute-done.7), kind=kLoop, calls=%fused_computation.6 | loop fusion | flops 143360 | bytes 245760 | tf_op jit(solution)/shard_map/convert_element_type | solution.py:350
  (6 shorter events, 0.1 us)
Async XLA Ops:
  1.5 17.6 %slice-start = ((s8[5242880]{0:T(1024)(128)(4,1)}), s8[4194304]{0:T(1024)(128)(4,1)S(1)}, s32[]{:S(2)}) async-start(s8[5242880]{0:T(1024)(128)(4,1)} %bitcast.6), calls=%async_computation | async-start | bytes 8388608
  1.5 17.6 %slice-start.2 = ((s8[5242880]{0:T(1024)(128)(4,1)}), s8[4194304]{0:T(1024)(128)(4,1)S(1)}, s32[]{:S(2)}) async-start(s8[5242880]{0:T(1024)(128)(4,1)} %bitcast.8), calls=%async_computation.2 | async-start | bytes 8388608
  1.6 9.9 %collective-permute-start.2 = (bf16[4,5248]{1,0:T(4,128)(2,1)S(1)}, bf16[4,5248]{1,0:T(4,128)(2,1)S(1)}, u32[]{:S(2)}, u32[]{:S(2)}) collective-permute-start(bf16[4,5248]{1,0:T(4,128)(2,1)S(1)} %pack.1.after_ref.refs_1_), channel_id=1, source_target_pairs={{0,12},{2,14},{4,8},{6,10},{8,4},{10,6},{12,0},{14,2},{1,13},{3,15... | collective-permute-start | bytes 125960 | tf_op jit(solution)/shard_map/ppermute | solution.py:18
  6.7 4.9 %collective-permute-start.1 = (bf16[4,5248]{1,0:T(4,128)(2,1)S(1)}, bf16[4,5248]{1,0:T(4,128)(2,1)S(1)}, u32[]{:S(2)}, u32[]{:S(2)}) collective-permute-start(bf16[4,5248]{1,0:T(4,128)(2,1)S(1)} %pack.1.after_ref.refs_1_), channel_id=1, source_target_pairs={{0,8},{2,10},{4,12},{6,14},{8,0},{10,2},{12,4},{14,6},{1,9},{3,11}... | collective-permute-start | bytes 125960 | tf_op jit(solution)/shard_map/ppermute | solution.py:18
  6.7 4.9 %collective-permute-start = (bf16[4,5248]{1,0:T(4,128)(2,1)S(1)}, bf16[4,5248]{1,0:T(4,128)(2,1)S(1)}, u32[]{:S(2)}, u32[]{:S(2)}) collective-permute-start(bf16[4,5248]{1,0:T(4,128)(2,1)S(1)} %pack.1.after_ref.refs_1_), channel_id=1, source_target_pairs={{0,4},{2,6},{4,0},{6,2},{8,12},{10,14},{12,8},{14,10},{1,5},{3,7},... | collective-permute-start | bytes 125960 | tf_op jit(solution)/shard_map/ppermute | solution.py:18
  11.6 7.5 %slice-start.1 = ((s8[5242880]{0:T(1024)(128)(4,1)}), s8[1048576]{0:T(1024)(128)(4,1)S(1)}, s32[]{:S(2)}) async-start(s8[5242880]{0:T(1024)(128)(4,1)} %bitcast.6), calls=%async_computation.1 | async-start | bytes 2097152
  11.6 7.5 %slice-start.3 = ((s8[5242880]{0:T(1024)(128)(4,1)}), s8[1048576]{0:T(1024)(128)(4,1)S(1)}, s32[]{:S(2)}) async-start(s8[5242880]{0:T(1024)(128)(4,1)} %bitcast.8), calls=%async_computation.3 | async-start | bytes 2097152
  11.7 5.7 %collective-permute-start.3 = (bf16[16,5248]{1,0:T(8,128)(2,1)S(1)}, bf16[16,5248]{1,0:T(8,128)(2,1)S(1)}, u32[]{:S(2)}, u32[]{:S(2)}) collective-permute-start(bf16[16,5248]{1,0:T(8,128)(2,1)S(1)} %join.2.after_ref.refs_1_), channel_id=1, source_target_pairs={{0,2},{2,0},{4,6},{6,4},{8,10},{10,8},{12,14},{14,12},{1,3},{3,1},... | collective-permute-start | bytes 503816 | tf_op jit(solution)/shard_map/ppermute | solution.py:18
  17.4 1.7 %collective-permute-start.4 = (bf16[32,5248]{1,0:T(8,128)(2,1)S(1)}, bf16[32,5248]{1,0:T(8,128)(2,1)S(1)}, u32[]{:S(2)}, u32[]{:S(2)}) collective-permute-start(bf16[32,5248]{1,0:T(8,128)(2,1)S(1)} %join.3.here_ref), channel_id=1, source_target_pairs={{0,1},{1,0},{2,3},{3,2},{4,5},{5,4},{6,7},{7,6},{8,9},{9,8},{10,11... | collective-permute-start | bytes 1007624 | tf_op jit(solution)/shard_map/ppermute | solution.py:22
  27.2 1.7 %collective-permute-start.5 = (bf16[32,5120]{1,0:T(8,128)(2,1)S(1)}, bf16[32,5120]{1,0:T(8,128)(2,1)S(1)}, u32[]{:S(2)}, u32[]{:S(2)}) collective-permute-start(bf16[32,5120]{1,0:T(8,128)(2,1)S(1)} %get-tuple-element.16), channel_id=1, source_target_pairs={{0,1},{1,0},{2,3},{3,2},{4,5},{5,4},{6,7},{7,6},{8,9},{9,8},{10,11... | collective-permute-start | bytes 983048 | tf_op jit(solution)/shard_map/ppermute | solution.py:22
  29.0 6.3 %collective-permute-start.6 = (bf16[16,5120]{1,0:T(8,128)(2,1)S(1)}, bf16[16,5120]{1,0:T(8,128)(2,1)S(1)}, u32[]{:S(2)}, u32[]{:S(2)}) collective-permute-start(bf16[16,5120]{1,0:T(8,128)(2,1)S(1)} %slice.43), channel_id=1, source_target_pairs={{0,2},{2,0},{4,6},{6,4},{8,10},{10,8},{12,14},{14,12},{1,3},{3,1},... | collective-permute-start | bytes 491528 | tf_op jit(solution)/shard_map/ppermute | solution.py:18
  35.4 4.2 %collective-permute-start.7 = (bf16[4,5120]{1,0:T(4,128)(2,1)S(1)}, bf16[4,5120]{1,0:T(4,128)(2,1)S(1)}, u32[]{:S(2)}, u32[]{:S(2)}) collective-permute-start(bf16[4,5120]{1,0:T(4,128)(2,1)S(1)} %get-tuple-element.19), channel_id=1, source_target_pairs={{0,4},{2,6},{4,0},{6,2},{8,12},{10,14},{12,8},{14,10},{1,5},{3,7},... | collective-permute-start | bytes 122888 | tf_op jit(solution)/shard_map/ppermute | solution.py:18
  36.7 6.1 %collective-permute-start.9 = (bf16[4,5120]{1,0:T(4,128)(2,1)S(1)}, bf16[4,5120]{1,0:T(4,128)(2,1)S(1)}, u32[]{:S(2)}, u32[]{:S(2)}) collective-permute-start(bf16[4,5120]{1,0:T(4,128)(2,1)S(1)} %get-tuple-element.20), channel_id=1, source_target_pairs={{0,12},{2,14},{4,8},{6,10},{8,4},{10,6},{12,0},{14,2},{1,13},{3,15... | collective-permute-start | bytes 122888 | tf_op jit(solution)/shard_map/ppermute | solution.py:18
  39.1 4.9 %collective-permute-start.8 = (bf16[4,5120]{1,0:T(4,128)(2,1)S(1)}, bf16[4,5120]{1,0:T(4,128)(2,1)S(1)}, u32[]{:S(2)}, u32[]{:S(2)}) collective-permute-start(bf16[4,5120]{1,0:T(4,128)(2,1)S(1)} %get-tuple-element.21), channel_id=1, source_target_pairs={{0,8},{2,10},{4,12},{6,14},{8,0},{10,2},{12,4},{14,6},{1,9},{3,11}... | collective-permute-start | bytes 122888 | tf_op jit(solution)/shard_map/ppermute | solution.py:18

commit v3 on v2

--- a/solution.py
+++ b/solution.py
@@ -10,7 +10,7 @@
 META = 128
 LANE = 128
 STEP = 512
-DOWN_CHUNK = 2560
+DOWN_CHUNK = 1280
 
 
 def expert_swap(x, bits):
@@ -174,14 +174,18 @@
     hot_out_ref,
     mine_ref,
     other_ref,
+    shared_hidden_ref,
+    cold_hidden_ref,
+    hot_hidden_ref,
+    gate_ref,
+    hot_out,
     far_spread_ref,
     hot_in,
-    hot_out,
     in_sems,
     out_sem,
     hid_ref,
 ):
-    width = mine_ref.shape[1]
+    width = here_ref.shape[1] - META
     narrow = lax.axis_index("narrow")
     expert = lax.axis_index("expert")
     half = here_ref.shape[0]
@@ -247,14 +251,32 @@
         parts = [hid_ref[i] for i in range(tiles // group)]
         return parts[0] if len(parts) == 1 else jnp.concatenate(parts, axis=1)
 
-    shared_hidden = hidden(shared_in, None)
-    cold_hidden = hidden(cold_in, cold_rows)
+    gate_ref[...] = jnp.broadcast_to(gate, gate_ref.shape)
+    shared_hidden_ref[...] = hidden(shared_in, None)
+    cold_hidden_ref[...] = hidden(cold_in, cold_rows)
     for copy in in_copies:
         copy.wait()
-    hot_hidden = hidden(hot_in, hot_rows)
+    hot_hidden_ref[...] = hidden(hot_in, hot_rows)
     out_copy.wait()
+    down_columns(
+        0,
+        (shared_hidden_ref, cold_hidden_ref, hot_hidden_ref),
+        gate_ref,
+        (shared_out, cold_out, hot_out),
+        mine_ref,
+        other_ref,
+    )
+
+
+def down_columns(first, hiddens, gate_ref, weights, mine_ref, other_ref):
+    half, width = mine_ref.shape
+    shared_hidden, cold_hidden, hot_hidden = (ref[...] for ref in hiddens)
+    shared_out, cold_out, hot_out = weights
+    gate = gate_ref[:, 0:1]
+
     def down(chunk, _):
-        columns = pl.ds(pl.multiple_of(chunk * DOWN_CHUNK, DOWN_CHUNK), DOWN_CHUNK)
+        columns = pl.ds(pl.multiple_of(first + chunk * DOWN_CHUNK, DOWN_CHUNK), DOWN_CHUNK)
+        stored = pl.ds(pl.multiple_of(chunk * DOWN_CHUNK, DOWN_CHUNK), DOWN_CHUNK)
         routed = jnp.dot(cold_hidden, cold_out[:, columns], preferred_element_type=jnp.float32)
         routed = routed + jnp.dot(
             hot_hidden, hot_out[:, columns], preferred_element_type=jnp.float32
@@ -262,11 +284,50 @@
         total = gate * routed + jnp.dot(
             shared_hidden, shared_out[:, columns], preferred_element_type=jnp.float32
         )
-        mine_ref[:, columns] = total[:half]
-        other_ref[:, columns] = total[half:].astype(jnp.bfloat16)
+        mine_ref[:, stored] = total[:half]
+        other_ref[:, stored] = total[half:].astype(jnp.bfloat16)
         return 0
 
     lax.fori_loop(0, width // DOWN_CHUNK, down, 0)
+
+
+def rest_kernel(
+    shared_hidden,
+    cold_hidden,
+    hot_hidden,
+    gate_ref,
+    shared_out,
+    cold_out,
+    hot_out,
+    mine_ref,
+    other_ref,
+):
+    down_columns(
+        shared_out.shape[1] - mine_ref.shape[1],
+        (shared_hidden, cold_hidden, hot_hidden),
+        gate_ref,
+        (shared_out, cold_out, hot_out),
+        mine_ref,
+        other_ref,
+    )
+
+
+def rest(hiddens, gate, weights):
+    half = gate.shape[0] // 2
+    columns = weights[0].shape[1] // 2
+    in_vmem = pl.BlockSpec(memory_space=pltpu.VMEM)
+    fixed = [pltpu.with_memory_space_constraint(w, pltpu.VMEM) for w in (*hiddens, gate)]
+    return pl.pallas_call(
+        rest_kernel,
+        out_shape=(
+            pltpu.VMEM((half, columns), jnp.float32),
+            pltpu.VMEM((half, columns), jnp.bfloat16),
+        ),
+        in_specs=[in_vmem] * 7,
+        out_specs=(in_vmem, in_vmem),
+        compiler_params=pltpu.CompilerParams(vmem_limit_bytes=4 << 20),
+        name="rest",
+    )(*fixed, weights[0], weights[1], pltpu.with_memory_space_constraint(weights[2], pltpu.VMEM))
 
 
 def layer(here, far, near_spread, weights, tok_rows):
@@ -278,22 +339,24 @@
     hot_used = hot_part // 2 if split_hot else hot_part
     in_vmem = pl.BlockSpec(memory_space=pltpu.VMEM)
     in_hbm = pl.BlockSpec(memory_space=pltpu.HBM)
-    held = 8 * half * width + 6 * hot_used * width
+    held = 8 * half * width + 4 * hot_used * width
     tiles = (shared_in.shape[0], cold_in.shape[0], hot_used // LANE)
     group = 2 if all(count % 2 == 0 for count in tiles) else 1
     most = max(tiles) // group
     return pl.pallas_call(
         functools.partial(layer_kernel, split_hot, tok_rows, lax.axis_size("expert")),
         out_shape=(
-            pltpu.VMEM((half, width), jnp.float32),
-            pltpu.VMEM((half, width), jnp.bfloat16),
+            pltpu.VMEM((half, width // 2), jnp.float32),
+            pltpu.VMEM((half, width // 2), jnp.bfloat16),
+            *(pltpu.VMEM((2 * half, count * LANE), jnp.bfloat16) for count in tiles),
+            pltpu.VMEM((2 * half, LANE), jnp.float32),
+            pltpu.VMEM((hot_used, width), jnp.bfloat16),
         ),
         in_specs=[in_vmem] * 5 + [in_hbm] + [in_vmem] * 2 + [in_hbm],
-        out_specs=(in_vmem, in_vmem),
+        out_specs=(in_vmem,) * 7,
         scratch_shapes=[
             pltpu.VMEM((2 * half, 2 * width), jnp.bfloat16),
             pltpu.VMEM((hot_used // LANE, 2 * width, LANE), jnp.bfloat16),
-            pltpu.VMEM((hot_used, width), jnp.bfloat16),
             pltpu.SemaphoreType.DMA((hot_used // LANE,)),
             pltpu.SemaphoreType.DMA,
             pltpu.VMEM((most, 2 * half, LANE * group), jnp.bfloat16),
@@ -339,10 +402,15 @@
     near_spread = spread_near(here)
     far = narrow_swap(here)
     weights = (shared_in, cold_in, hot_gate_up, shared_down, cold_down[0], hot_down)
-    mine, other = layer(here, far, near_spread, weights, tok_rows)
-    mine = mine + narrow_swap(other).astype(jnp.float32)
+    first, first_other, *hiddens, gate, hot_out = layer(here, far, near_spread, weights, tok_rows)
+    second, second_other = rest(hiddens, gate, (shared_down, cold_down[0], hot_out))
     part = tok_rows * high
-    mine = mine[:part] + expert_swap(mine[part:].astype(jnp.bfloat16), 1).astype(jnp.float32)
+    halves = []
+    for mine, other in ((first, first_other), (second, second_other)):
+        mine = mine + narrow_swap(other).astype(jnp.float32)
+        low = expert_swap(mine[part:].astype(jnp.bfloat16), 1)
+        halves.append(mine[:part] + low.astype(jnp.float32))
+    mine = jnp.concatenate(halves, axis=1)
     total = mine[:tok_rows]
     for step in range(1, high):
         block = mine[step * tok_rows : (step + 1) * tok_rows].astype(jnp.bfloat16)

time: 44.9 us -> 44.1 us (0.982)
  waiting for transfers between devices: 11.9 us -> 9.32 us
  starting transfers between devices: 13.2 us -> 14.6 us
    ppermute x2 -> x3, waiting for transfers between devices: 2.3 us -> 0.81 us  [narrow_swap(): return lax.ppermute(x, 'narrow', [(0, 1), (1, 0)])]
    pallas_call x0 -> x1, Pallas kernels: none -> 1.43 us  [rest(): pl.pallas_call(rest_kernel, out_shape=(pltpu.VMEM((half, columns), jnp.fl...]
    pallas_call x1, Pallas kernels: 8.02 us -> 6.92 us  [layer(): pl.pallas_call(functools.partial(layer_kernel, split_hot, tok_rows, lax.a...]
    ppermute x8 -> x9, waiting for transfers between devices: 9.57 us -> 8.51 us  [expert_swap(): return lax.ppermute(x, 'expert', [(i, i ^ bits) for i in range(size)])]
    ppermute x8 -> x9, starting transfers between devices: 12.9 us -> 13.9 us  [expert_swap(): return lax.ppermute(x, 'expert', [(i, i ^ bits) for i in range(size)])]
  transfers between devices with their start and end apart: 10 -> 12, of which waited for: 6 -> 6; matrix products, arithmetic and copies ran while one was open for 0% -> 0% of each run, Pallas kernels for 20% -> 24%
where the time goes in v3:
time: 44.1 us; the launch traced here: 43.9 us
  Pallas kernels  18.3 us (41%)
  starting transfers between devices  14.6 us (33%)
  waiting for transfers between devices  9.32 us (21%)
  between operations  0.83 us (2%)
  other arithmetic  0.78 us (2%)
    ppermute x9, starting transfers between devices, expert_swap(): return lax.ppermute(x, 'expert', [(i, i ^ bits) for i in range(size)])  13.9 us
    ppermute x9, waiting for transfers between devices, expert_swap(): return lax.ppermute(x, 'expert', [(i, i ^ bits) for i in range(size)])  8.51 us
    pallas_call x2, Pallas kernels, fetch(): pl.pallas_call(fetch_kernel, out_shape=(pltpu.VMEM((part // LANE, 2 * wid...  8.19 us
    pallas_call x1, Pallas kernels, layer(): pl.pallas_call(functools.partial(layer_kernel, split_hot, tok_rows, lax.a...  6.92 us
    pallas_call x1, Pallas kernels, rest(): pl.pallas_call(rest_kernel, out_shape=(pltpu.VMEM((half, columns), jnp.fl...  1.43 us
  transfers between devices with their start and end apart: 12, of which 6 were waited for; matrix products, arithmetic and copies ran while one was open for 0% of the time, Pallas kernels for 24%

profile of v3, /device:TPU:0, one launch (start us, length us, event | category | flops | bytes accessed | tf_op | source)
XLA Modules:
  0.0 43.9 jit_solution(17592535947690088491)
XLA Ops:
  0.7 0.9 %pack.1.after_ref.refs_1_ = bf16[4,5248]{1,0:T(4,128)(2,1)S(1)} custom-call(bf16[4,5120]{1,0:T(4,128)(2,1)} %tokens_ref.1, s32[1,4]{1,0:T(1,128)} %bitcast.12, s32[1,4]{1,0:T(1,128)} %bitcast.13, bf16[1,4]{1,0:T(2,128)(2,1)} %bitcast.14, s32[1,1]{1,0:T(1,128)} %bitcast.5.capacity_ref), custom_call_target="tpu_custom_call" | custom-call | tf_op jit(solution)/shard_map/pack/pallas_call | solution.py:56
  1.5 0.0 slice-start
  1.5 0.0 slice-start.2
  1.6 5.1 %collective-permute-start.2 = (bf16[4,5248]{1,0:T(4,128)(2,1)S(1)}, bf16[4,5248]{1,0:T(4,128)(2,1)S(1)}, u32[]{:S(2)}, u32[]{:S(2)}) collective-permute-start(bf16[4,5248]{1,0:T(4,128)(2,1)S(1)} %pack.1.after_ref.refs_1_), channel_id=1, source_target_pairs={{0,12},{2,14},{4,8},{6,10},{8,4},{10,6},{12,0},{14,2},{1,13},{3,15... | collective-permute-start | bytes 125960 | tf_op jit(solution)/shard_map/ppermute | solution.py:18
  6.7 0.0 collective-permute-start.1
  6.7 0.6 %collective-permute-start = (bf16[4,5248]{1,0:T(4,128)(2,1)S(1)}, bf16[4,5248]{1,0:T(4,128)(2,1)S(1)}, u32[]{:S(2)}, u32[]{:S(2)}) collective-permute-start(bf16[4,5248]{1,0:T(4,128)(2,1)S(1)} %pack.1.after_ref.refs_1_), channel_id=1, source_target_pairs={{0,4},{2,6},{4,0},{6,2},{8,12},{10,14},{12,8},{14,10},{1,5},{3,7},... | collective-permute-start | bytes 125960 | tf_op jit(solution)/shard_map/ppermute | solution.py:18
  7.3 4.1 %fetch.2 = (bf16[4,10240,128]{2,1,0:T(8,128)(2,1)S(1)}, f32[8,128]{1,0:T(8,128)S(1)}) custom-call(bf16[5120,2,512]{2,1,0:T(2,128)(2,1)} %source_ref.2, bf16[4,5248]{1,0:T(4,128)(2,1)S(1)} %pack.1.after_ref.refs_1_), custom_call_target="tpu_custom_call" | custom-call | bytes 20971520 | tf_op jit(solution)/shard_map/fetch/pallas_call | solution.py:130
  11.4 0.0 collective-permute-done.2.refs_4_
  11.4 0.2 collective-permute-done.1.refs_3_
  11.6 0.0 collective-permute-done.refs_2_
  11.6 0.0 slice-start.1
  11.6 0.0 slice-start.3
  11.7 1.6 %collective-permute-start.3 = (bf16[16,5248]{1,0:T(8,128)(2,1)S(1)}, bf16[16,5248]{1,0:T(8,128)(2,1)S(1)}, u32[]{:S(2)}, u32[]{:S(2)}) collective-permute-start(bf16[16,5248]{1,0:T(8,128)(2,1)S(1)} %join.2.after_ref.refs_1_), channel_id=1, source_target_pairs={{0,2},{2,0},{4,6},{6,4},{8,10},{10,8},{12,14},{14,12},{1,3},{3,1},... | collective-permute-start | bytes 503816 | tf_op jit(solution)/shard_map/ppermute | solution.py:18
  13.3 4.1 %fetch.3 = (bf16[4,10240,128]{2,1,0:T(8,128)(2,1)S(1)}, f32[8,128]{1,0:T(8,128)S(1)}) custom-call(bf16[1,5120,2,512]{3,2,1,0:T(2,128)(2,1)} %source_ref.3, bf16[16,5248]{1,0:T(8,128)(2,1)S(1)} %join.2.after_ref.refs_1_), custom_call_target="tpu_custom_call" | custom-call | bytes 20971520 | tf_op jit(solution)/shard_map/fetch/pallas_call | solution.py:130
  17.4 0.0 collective-permute-done.3.refs_2_
  17.4 0.1 collective-permute-start.4
  17.5 0.8 %spread.1.near_spread_ref = bf16[64,10240]{1,0:T(8,128)(2,1)S(1)} custom-call(bf16[32,5248]{1,0:T(8,128)(2,1)S(1)} %join.3.here_ref), custom_call_target="tpu_custom_call" | custom-call | tf_op jit(solution)/shard_map/spread/pallas_call | solution.py:152
  18.3 0.8 %collective-permute-done.4.far_ref = bf16[32,5248]{1,0:T(8,128)(2,1)S(1)} collective-permute-done((bf16[32,5248]{1,0:T(8,128)(2,1)S(1)}, bf16[32,5248]{1,0:T(8,128)(2,1)S(1)}, u32[]{:S(2)}, u32[]{:S(2)}) %collective-permute-start.4) | collective-permute-done | bytes 335904 | tf_op jit(solution)/shard_map/ppermute | solution.py:22
  19.1 0.0 slice-done
  19.1 0.0 slice-done.2
  19.1 0.0 slice-done.1
  19.1 0.0 slice-done.3
  19.1 6.9 %layer.1 = (f32[32,2560]{1,0:T(8,128)S(1)}, bf16[32,2560]{1,0:T(8,128)(2,1)S(1)}, bf16[64,512]{1,0:T(8,128)(2,1)S(1)}, bf16[64,512]{1,0:T(8,128)(2,1)S(1)}, bf16...) custom-call(bf16[32,5248]{1,0:T(8,128)(2,1)S(1)} %join.3.here_ref, ...), custom_call_target="tpu_custom_call" | custom-call | tf_op jit(solution)/shard_map/layer/pallas_call | solution.py:346
  26.1 0.2 collective-permute-start.5
  26.3 1.4 %rest.1 = (f32[32,2560]{1,0:T(8,128)S(1)}, bf16[32,2560]{1,0:T(8,128)(2,1)S(1)}) custom-call(bf16[64,512]{1,0:T(8,128)(2,1)S(1)} %get-tuple-element.24.shared_hidden, bf16[64,512]{1,0:T(8,128)(2,1)S(1)} %get-tuple-element.25.cold_hidden, bf16[64,256]{1,0:T(8,128)(2,1)S(1)} %get-tuple-element.26.hot_hidden, f32[64,128]{1,0:T(8,128)S(1)} %get-tuple-element.27.gate_ref, ...), custom_call_target="tpu_custom_call" | custom-call | tf_op jit(solution)/shard_map/rest/pallas_call | solution.py:320
  27.7 0.4 %collective-permute-start.7 = (bf16[32,2560]{1,0:T(8,128)(2,1)S(1)}, bf16[32,2560]{1,0:T(8,128)(2,1)S(1)}, u32[]{:S(2)}, u32[]{:S(2)}) collective-permute-start(bf16[32,2560]{1,0:T(8,128)(2,1)S(1)} %get-tuple-element.30), channel_id=1, source_target_pairs={{0,1},{1,0},{2,3},{3,2},{4,5},{5,4},{6,7},{7,6},{8,9},{9,8},{10,11... | collective-permute-start | bytes 491528 | tf_op jit(solution)/shard_map/ppermute | solution.py:22
  28.1 0.0 collective-permute-done.5
  28.2 1.3 %collective-permute-start.6 = (bf16[16,2560]{1,0:T(8,128)(2,1)S(1)}, bf16[16,2560]{1,0:T(8,128)(2,1)S(1)}, u32[]{:S(2)}, u32[]{:S(2)}) collective-permute-start(bf16[16,2560]{1,0:T(8,128)(2,1)S(1)} %slice.67), channel_id=1, source_target_pairs={{0,2},{2,0},{4,6},{6,4},{8,10},{10,8},{12,14},{14,12},{1,3},{3,1},... | collective-permute-start | bytes 245768 | tf_op jit(solution)/shard_map/ppermute | solution.py:18
  29.5 0.0 collective-permute-done.7
  29.6 1.0 %collective-permute-start.8 = (bf16[16,2560]{1,0:T(8,128)(2,1)S(1)}, bf16[16,2560]{1,0:T(8,128)(2,1)S(1)}, u32[]{:S(2)}, u32[]{:S(2)}) collective-permute-start(bf16[16,2560]{1,0:T(8,128)(2,1)S(1)} %slice.66), channel_id=1, source_target_pairs={{0,2},{2,0},{4,6},{6,4},{8,10},{10,8},{12,14},{14,12},{1,3},{3,1},... | collective-permute-start | bytes 245768 | tf_op jit(solution)/shard_map/ppermute | solution.py:18
  30.6 2.8 %collective-permute-done.6 = bf16[16,2560]{1,0:T(8,128)(2,1)S(1)} collective-permute-done((bf16[16,2560]{1,0:T(8,128)(2,1)S(1)}, bf16[16,2560]{1,0:T(8,128)(2,1)S(1)}, u32[]{:S(2)}, u32[]{:S(2)}) %collective-permute-start.6) | collective-permute-done | bytes 81952 | tf_op jit(solution)/shard_map/ppermute | solution.py:18
  33.4 1.2 %collective-permute-done.8 = bf16[16,2560]{1,0:T(8,128)(2,1)S(1)} collective-permute-done((bf16[16,2560]{1,0:T(8,128)(2,1)S(1)}, bf16[16,2560]{1,0:T(8,128)(2,1)S(1)}, u32[]{:S(2)}, u32[]{:S(2)}) %collective-permute-start.8) | collective-permute-done | bytes 81952 | tf_op jit(solution)/shard_map/ppermute | solution.py:18
  34.6 0.1 fusion.6
  34.6 1.3 %collective-permute-start.9 = (bf16[4,5120]{1,0:T(4,128)(2,1)S(1)}, bf16[4,5120]{1,0:T(4,128)(2,1)S(1)}, u32[]{:S(2)}, u32[]{:S(2)}) collective-permute-start(bf16[4,5120]{1,0:T(4,128)(2,1)S(1)} %get-tuple-element.31), channel_id=1, source_target_pairs={{0,4},{2,6},{4,0},{6,2},{8,12},{10,14},{12,8},{14,10},{1,5},{3,7},... | collective-permute-start | bytes 122888 | tf_op jit(solution)/shard_map/ppermute | solution.py:18
  35.9 2.4 %collective-permute-start.11 = (bf16[4,5120]{1,0:T(4,128)(2,1)S(1)}, bf16[4,5120]{1,0:T(4,128)(2,1)S(1)}, u32[]{:S(2)}, u32[]{:S(2)}) collective-permute-start(bf16[4,5120]{1,0:T(4,128)(2,1)S(1)} %get-tuple-element.32), channel_id=1, source_target_pairs={{0,12},{2,14},{4,8},{6,10},{8,4},{10,6},{12,0},{14,2},{1,13},{3,15... | collective-permute-start | bytes 122888 | tf_op jit(solution)/shard_map/ppermute | solution.py:18
  38.4 0.5 %collective-permute-start.10 = (bf16[4,5120]{1,0:T(4,128)(2,1)S(1)}, bf16[4,5120]{1,0:T(4,128)(2,1)S(1)}, u32[]{:S(2)}, u32[]{:S(2)}) collective-permute-start(bf16[4,5120]{1,0:T(4,128)(2,1)S(1)} %get-tuple-element.33), channel_id=1, source_target_pairs={{0,8},{2,10},{4,12},{6,14},{8,0},{10,2},{12,4},{14,6},{1,9},{3,11}... | collective-permute-start | bytes 122888 | tf_op jit(solution)/shard_map/ppermute | solution.py:18
  38.8 0.0 collective-permute-done.9
  38.9 3.4 %collective-permute-done.11 = bf16[4,5120]{1,0:T(4,128)(2,1)S(1)} collective-permute-done((bf16[4,5120]{1,0:T(4,128)(2,1)S(1)}, bf16[4,5120]{1,0:T(4,128)(2,1)S(1)}, u32[]{:S(2)}, u32[]{:S(2)}) %collective-permute-start.11) | collective-permute-done | bytes 40992 | tf_op jit(solution)/shard_map/ppermute | solution.py:18
  42.2 1.0 %collective-permute-done.10 = bf16[4,5120]{1,0:T(4,128)(2,1)S(1)} collective-permute-done((bf16[4,5120]{1,0:T(4,128)(2,1)S(1)}, bf16[4,5120]{1,0:T(4,128)(2,1)S(1)}, u32[]{:S(2)}, u32[]{:S(2)}) %collective-permute-start.10) | collective-permute-done | bytes 40992 | tf_op jit(solution)/shard_map/ppermute | solution.py:18
  43.3 0.7 %fusion.5 = bf16[4,5120]{1,0:T(4,128)(2,1)} fusion(bf16[4,5120]{1,0:T(4,128)(2,1)S(1)} %collective-permute-done.11, bf16[4,5120]{1,0:T(4,128)(2,1)S(1)} %collective-permute-done.10, bf16[4,5120]{1,0:T(4,128)(2,1)S(1)} %collective-permute-done.9, f32[16,2560]{1,0:T(8,128)S(1)} %slice_add_fusion, f32[16,2560]{1,0:T(8,128)S(1)} %slice_add_fusion.1), kind=kLoop, calls=%fused_computation.14 | loop fusion | flops 163840 | bytes 491520 | tf_op jit(solution)/shard_map/convert_element_type | solution.py:418
  (11 shorter events, 0.2 us)
Async XLA Ops:
  1.5 17.6 %slice-start = ((s8[5242880]{0:T(1024)(128)(4,1)}), s8[4194304]{0:T(1024)(128)(4,1)S(1)}, s32[]{:S(2)}) async-start(s8[5242880]{0:T(1024)(128)(4,1)} %bitcast.6), calls=%async_computation | async-start | bytes 8388608
  1.5 17.6 %slice-start.2 = ((s8[5242880]{0:T(1024)(128)(4,1)}), s8[4194304]{0:T(1024)(128)(4,1)S(1)}, s32[]{:S(2)}) async-start(s8[5242880]{0:T(1024)(128)(4,1)} %bitcast.8), calls=%async_computation.2 | async-start | bytes 8388608
  1.6 9.9 %collective-permute-start.2 = (bf16[4,5248]{1,0:T(4,128)(2,1)S(1)}, bf16[4,5248]{1,0:T(4,128)(2,1)S(1)}, u32[]{:S(2)}, u32[]{:S(2)}) collective-permute-start(bf16[4,5248]{1,0:T(4,128)(2,1)S(1)} %pack.1.after_ref.refs_1_), channel_id=1, source_target_pairs={{0,12},{2,14},{4,8},{6,10},{8,4},{10,6},{12,0},{14,2},{1,13},{3,15... | collective-permute-start | bytes 125960 | tf_op jit(solution)/shard_map/ppermute | solution.py:18
  6.7 4.9 %collective-permute-start.1 = (bf16[4,5248]{1,0:T(4,128)(2,1)S(1)}, bf16[4,5248]{1,0:T(4,128)(2,1)S(1)}, u32[]{:S(2)}, u32[]{:S(2)}) collective-permute-start(bf16[4,5248]{1,0:T(4,128)(2,1)S(1)} %pack.1.after_ref.refs_1_), channel_id=1, source_target_pairs={{0,8},{2,10},{4,12},{6,14},{8,0},{10,2},{12,4},{14,6},{1,9},{3,11}... | collective-permute-start | bytes 125960 | tf_op jit(solution)/shard_map/ppermute | solution.py:18
  6.7 4.9 %collective-permute-start = (bf16[4,5248]{1,0:T(4,128)(2,1)S(1)}, bf16[4,5248]{1,0:T(4,128)(2,1)S(1)}, u32[]{:S(2)}, u32[]{:S(2)}) collective-permute-start(bf16[4,5248]{1,0:T(4,128)(2,1)S(1)} %pack.1.after_ref.refs_1_), channel_id=1, source_target_pairs={{0,4},{2,6},{4,0},{6,2},{8,12},{10,14},{12,8},{14,10},{1,5},{3,7},... | collective-permute-start | bytes 125960 | tf_op jit(solution)/shard_map/ppermute | solution.py:18
  11.6 7.5 %slice-start.1 = ((s8[5242880]{0:T(1024)(128)(4,1)}), s8[1048576]{0:T(1024)(128)(4,1)S(1)}, s32[]{:S(2)}) async-start(s8[5242880]{0:T(1024)(128)(4,1)} %bitcast.6), calls=%async_computation.1 | async-start | bytes 2097152
  11.6 7.5 %slice-start.3 = ((s8[5242880]{0:T(1024)(128)(4,1)}), s8[1048576]{0:T(1024)(128)(4,1)S(1)}, s32[]{:S(2)}) async-start(s8[5242880]{0:T(1024)(128)(4,1)} %bitcast.8), calls=%async_computation.3 | async-start | bytes 2097152
  11.7 5.7 %collective-permute-start.3 = (bf16[16,5248]{1,0:T(8,128)(2,1)S(1)}, bf16[16,5248]{1,0:T(8,128)(2,1)S(1)}, u32[]{:S(2)}, u32[]{:S(2)}) collective-permute-start(bf16[16,5248]{1,0:T(8,128)(2,1)S(1)} %join.2.after_ref.refs_1_), channel_id=1, source_target_pairs={{0,2},{2,0},{4,6},{6,4},{8,10},{10,8},{12,14},{14,12},{1,3},{3,1},... | collective-permute-start | bytes 503816 | tf_op jit(solution)/shard_map/ppermute | solution.py:18
  17.4 1.7 %collective-permute-start.4 = (bf16[32,5248]{1,0:T(8,128)(2,1)S(1)}, bf16[32,5248]{1,0:T(8,128)(2,1)S(1)}, u32[]{:S(2)}, u32[]{:S(2)}) collective-permute-start(bf16[32,5248]{1,0:T(8,128)(2,1)S(1)} %join.3.here_ref), channel_id=1, source_target_pairs={{0,1},{1,0},{2,3},{3,2},{4,5},{5,4},{6,7},{7,6},{8,9},{9,8},{10,11... | collective-permute-start | bytes 1007624 | tf_op jit(solution)/shard_map/ppermute | solution.py:22
  26.1 2.1 %collective-permute-start.5 = (bf16[32,2560]{1,0:T(8,128)(2,1)S(1)}, bf16[32,2560]{1,0:T(8,128)(2,1)S(1)}, u32[]{:S(2)}, u32[]{:S(2)}) collective-permute-start(bf16[32,2560]{1,0:T(8,128)(2,1)S(1)} %get-tuple-element.23), channel_id=1, source_target_pairs={{0,1},{1,0},{2,3},{3,2},{4,5},{5,4},{6,7},{7,6},{8,9},{9,8},{10,11... | collective-permute-start | bytes 491528 | tf_op jit(solution)/shard_map/ppermute | solution.py:22
  27.7 1.8 %collective-permute-start.7 = (bf16[32,2560]{1,0:T(8,128)(2,1)S(1)}, bf16[32,2560]{1,0:T(8,128)(2,1)S(1)}, u32[]{:S(2)}, u32[]{:S(2)}) collective-permute-start(bf16[32,2560]{1,0:T(8,128)(2,1)S(1)} %get-tuple-element.30), channel_id=1, source_target_pairs={{0,1},{1,0},{2,3},{3,2},{4,5},{5,4},{6,7},{7,6},{8,9},{9,8},{10,11... | collective-permute-start | bytes 491528 | tf_op jit(solution)/shard_map/ppermute | solution.py:22
  28.2 5.1 %collective-permute-start.6 = (bf16[16,2560]{1,0:T(8,128)(2,1)S(1)}, bf16[16,2560]{1,0:T(8,128)(2,1)S(1)}, u32[]{:S(2)}, u32[]{:S(2)}) collective-permute-start(bf16[16,2560]{1,0:T(8,128)(2,1)S(1)} %slice.67), channel_id=1, source_target_pairs={{0,2},{2,0},{4,6},{6,4},{8,10},{10,8},{12,14},{14,12},{1,3},{3,1},... | collective-permute-start | bytes 245768 | tf_op jit(solution)/shard_map/ppermute | solution.py:18
  29.6 4.9 %collective-permute-start.8 = (bf16[16,2560]{1,0:T(8,128)(2,1)S(1)}, bf16[16,2560]{1,0:T(8,128)(2,1)S(1)}, u32[]{:S(2)}, u32[]{:S(2)}) collective-permute-start(bf16[16,2560]{1,0:T(8,128)(2,1)S(1)} %slice.66), channel_id=1, source_target_pairs={{0,2},{2,0},{4,6},{6,4},{8,10},{10,8},{12,14},{14,12},{1,3},{3,1},... | collective-permute-start | bytes 245768 | tf_op jit(solution)/shard_map/ppermute | solution.py:18
  34.6 4.2 %collective-permute-start.9 = (bf16[4,5120]{1,0:T(4,128)(2,1)S(1)}, bf16[4,5120]{1,0:T(4,128)(2,1)S(1)}, u32[]{:S(2)}, u32[]{:S(2)}) collective-permute-start(bf16[4,5120]{1,0:T(4,128)(2,1)S(1)} %get-tuple-element.31), channel_id=1, source_target_pairs={{0,4},{2,6},{4,0},{6,2},{8,12},{10,14},{12,8},{14,10},{1,5},{3,7},... | collective-permute-start | bytes 122888 | tf_op jit(solution)/shard_map/ppermute | solution.py:18
  35.9 6.3 %collective-permute-start.11 = (bf16[4,5120]{1,0:T(4,128)(2,1)S(1)}, bf16[4,5120]{1,0:T(4,128)(2,1)S(1)}, u32[]{:S(2)}, u32[]{:S(2)}) collective-permute-start(bf16[4,5120]{1,0:T(4,128)(2,1)S(1)} %get-tuple-element.32), channel_id=1, source_target_pairs={{0,12},{2,14},{4,8},{6,10},{8,4},{10,6},{12,0},{14,2},{1,13},{3,15... | collective-permute-start | bytes 122888 | tf_op jit(solution)/shard_map/ppermute | solution.py:18
  38.4 4.9 %collective-permute-start.10 = (bf16[4,5120]{1,0:T(4,128)(2,1)S(1)}, bf16[4,5120]{1,0:T(4,128)(2,1)S(1)}, u32[]{:S(2)}, u32[]{:S(2)}) collective-permute-start(bf16[4,5120]{1,0:T(4,128)(2,1)S(1)} %get-tuple-element.33), channel_id=1, source_target_pairs={{0,8},{2,10},{4,12},{6,14},{8,0},{10,2},{12,4},{14,6},{1,9},{3,11}... | collective-permute-start | bytes 122888 | tf_op jit(solution)/shard_map/ppermute | solution.py:18

commit v4 on v3

--- a/solution.py
+++ b/solution.py
@@ -268,15 +268,15 @@
     )
 
 
-def down_columns(first, hiddens, gate_ref, weights, mine_ref, other_ref):
+def down_columns(first, hiddens, gate_ref, weights, mine_ref, other_ref, size=DOWN_CHUNK):
     half, width = mine_ref.shape
     shared_hidden, cold_hidden, hot_hidden = (ref[...] for ref in hiddens)
     shared_out, cold_out, hot_out = weights
     gate = gate_ref[:, 0:1]
 
     def down(chunk, _):
-        columns = pl.ds(pl.multiple_of(first + chunk * DOWN_CHUNK, DOWN_CHUNK), DOWN_CHUNK)
-        stored = pl.ds(pl.multiple_of(chunk * DOWN_CHUNK, DOWN_CHUNK), DOWN_CHUNK)
+        columns = pl.ds(pl.multiple_of(first + chunk * size, size), size)
+        stored = pl.ds(pl.multiple_of(chunk * size, size), size)
         routed = jnp.dot(cold_hidden, cold_out[:, columns], preferred_element_type=jnp.float32)
         routed = routed + jnp.dot(
             hot_hidden, hot_out[:, columns], preferred_element_type=jnp.float32
@@ -288,7 +288,7 @@
         other_ref[:, stored] = total[half:].astype(jnp.bfloat16)
         return 0
 
-    lax.fori_loop(0, width // DOWN_CHUNK, down, 0)
+    lax.fori_loop(0, width // size, down, 0)
 
 
 def rest_kernel(
@@ -309,6 +309,7 @@
         (shared_out, cold_out, hot_out),
         mine_ref,
         other_ref,
+        mine_ref.shape[1],
     )
 
 

time: 44.1 us -> 43.9 us (level)
  transfers between devices with their start and end apart: 12 -> 12, of which waited for: 6 -> 6; matrix products, arithmetic and copies ran while one was open for 0% -> 0% of each run, Pallas kernels for 24% -> 23%
where the time goes in v4:
time: 43.9 us; the launch traced here: 43.7 us
  Pallas kernels  18.1 us (41%)
  starting transfers between devices  14.6 us (33%)
  waiting for transfers between devices  9.32 us (21%)
  between operations  0.83 us (2%)
  other arithmetic  0.78 us (2%)
    ppermute x9, starting transfers between devices, expert_swap(): return lax.ppermute(x, 'expert', [(i, i ^ bits) for i in range(size)])  13.9 us
    ppermute x9, waiting for transfers between devices, expert_swap(): return lax.ppermute(x, 'expert', [(i, i ^ bits) for i in range(size)])  8.51 us
    pallas_call x2, Pallas kernels, fetch(): pl.pallas_call(fetch_kernel, out_shape=(pltpu.VMEM((part // LANE, 2 * wid...  8.19 us
    pallas_call x1, Pallas kernels, layer(): pl.pallas_call(functools.partial(layer_kernel, split_hot, tok_rows, lax.a...  6.92 us
    pallas_call x1, Pallas kernels, rest(): pl.pallas_call(rest_kernel, out_shape=(pltpu.VMEM((half, columns), jnp.fl...  1.26 us
    pallas_call x1, Pallas kernels, pack(): pl.pallas_call(pack_kernel, out_shape=pltpu.VMEM((rows, width + META), jn...  0.88 us
  transfers between devices with their start and end apart: 12, of which 6 were waited for; matrix products, arithmetic and copies ran while one was open for 0% of the time, Pallas kernels for 23%

profile of v4, /device:TPU:0, one launch (start us, length us, event | category | flops | bytes accessed | tf_op | source)
XLA Modules:
  0.0 43.7 jit_solution(15641250603849900325)
XLA Ops:
  0.7 0.9 %pack.1.after_ref.refs_1_ = bf16[4,5248]{1,0:T(4,128)(2,1)S(1)} custom-call(bf16[4,5120]{1,0:T(4,128)(2,1)} %tokens_ref.1, s32[1,4]{1,0:T(1,128)} %bitcast.12, s32[1,4]{1,0:T(1,128)} %bitcast.13, bf16[1,4]{1,0:T(2,128)(2,1)} %bitcast.14, s32[1,1]{1,0:T(1,128)} %bitcast.5.capacity_ref), custom_call_target="tpu_custom_call" | custom-call | tf_op jit(solution)/shard_map/pack/pallas_call | solution.py:56
  1.5 0.0 slice-start
  1.5 0.0 slice-start.2
  1.6 5.1 %collective-permute-start.2 = (bf16[4,5248]{1,0:T(4,128)(2,1)S(1)}, bf16[4,5248]{1,0:T(4,128)(2,1)S(1)}, u32[]{:S(2)}, u32[]{:S(2)}) collective-permute-start(bf16[4,5248]{1,0:T(4,128)(2,1)S(1)} %pack.1.after_ref.refs_1_), channel_id=1, source_target_pairs={{0,12},{2,14},{4,8},{6,10},{8,4},{10,6},{12,0},{14,2},{1,13},{3,15... | collective-permute-start | bytes 125960 | tf_op jit(solution)/shard_map/ppermute | solution.py:18
  6.7 0.0 collective-permute-start.1
  6.7 0.6 %collective-permute-start = (bf16[4,5248]{1,0:T(4,128)(2,1)S(1)}, bf16[4,5248]{1,0:T(4,128)(2,1)S(1)}, u32[]{:S(2)}, u32[]{:S(2)}) collective-permute-start(bf16[4,5248]{1,0:T(4,128)(2,1)S(1)} %pack.1.after_ref.refs_1_), channel_id=1, source_target_pairs={{0,4},{2,6},{4,0},{6,2},{8,12},{10,14},{12,8},{14,10},{1,5},{3,7},... | collective-permute-start | bytes 125960 | tf_op jit(solution)/shard_map/ppermute | solution.py:18
  7.3 4.1 %fetch.2 = (bf16[4,10240,128]{2,1,0:T(8,128)(2,1)S(1)}, f32[8,128]{1,0:T(8,128)S(1)}) custom-call(bf16[5120,2,512]{2,1,0:T(2,128)(2,1)} %source_ref.2, bf16[4,5248]{1,0:T(4,128)(2,1)S(1)} %pack.1.after_ref.refs_1_), custom_call_target="tpu_custom_call" | custom-call | bytes 20971520 | tf_op jit(solution)/shard_map/fetch/pallas_call | solution.py:130
  11.4 0.0 collective-permute-done.2.refs_4_
  11.4 0.2 collective-permute-done.1.refs_3_
  11.6 0.0 collective-permute-done.refs_2_
  11.6 0.0 slice-start.1
  11.6 0.0 slice-start.3
  11.7 1.6 %collective-permute-start.3 = (bf16[16,5248]{1,0:T(8,128)(2,1)S(1)}, bf16[16,5248]{1,0:T(8,128)(2,1)S(1)}, u32[]{:S(2)}, u32[]{:S(2)}) collective-permute-start(bf16[16,5248]{1,0:T(8,128)(2,1)S(1)} %join.2.after_ref.refs_1_), channel_id=1, source_target_pairs={{0,2},{2,0},{4,6},{6,4},{8,10},{10,8},{12,14},{14,12},{1,3},{3,1},... | collective-permute-start | bytes 503816 | tf_op jit(solution)/shard_map/ppermute | solution.py:18
  13.3 4.1 %fetch.3 = (bf16[4,10240,128]{2,1,0:T(8,128)(2,1)S(1)}, f32[8,128]{1,0:T(8,128)S(1)}) custom-call(bf16[1,5120,2,512]{3,2,1,0:T(2,128)(2,1)} %source_ref.3, bf16[16,5248]{1,0:T(8,128)(2,1)S(1)} %join.2.after_ref.refs_1_), custom_call_target="tpu_custom_call" | custom-call | bytes 20971520 | tf_op jit(solution)/shard_map/fetch/pallas_call | solution.py:130
  17.4 0.0 collective-permute-done.3.refs_2_
  17.4 0.1 collective-permute-start.4
  17.5 0.8 %spread.1.near_spread_ref = bf16[64,10240]{1,0:T(8,128)(2,1)S(1)} custom-call(bf16[32,5248]{1,0:T(8,128)(2,1)S(1)} %join.3.here_ref), custom_call_target="tpu_custom_call" | custom-call | tf_op jit(solution)/shard_map/spread/pallas_call | solution.py:152
  18.3 0.8 %collective-permute-done.4.far_ref = bf16[32,5248]{1,0:T(8,128)(2,1)S(1)} collective-permute-done((bf16[32,5248]{1,0:T(8,128)(2,1)S(1)}, bf16[32,5248]{1,0:T(8,128)(2,1)S(1)}, u32[]{:S(2)}, u32[]{:S(2)}) %collective-permute-start.4) | collective-permute-done | bytes 335904 | tf_op jit(solution)/shard_map/ppermute | solution.py:22
  19.1 0.0 slice-done
  19.1 0.0 slice-done.2
  19.1 0.0 slice-done.1
  19.1 0.0 slice-done.3
  19.1 6.9 %layer.1 = (f32[32,2560]{1,0:T(8,128)S(1)}, bf16[32,2560]{1,0:T(8,128)(2,1)S(1)}, bf16[64,512]{1,0:T(8,128)(2,1)S(1)}, bf16[64,512]{1,0:T(8,128)(2,1)S(1)}, bf16...) custom-call(bf16[32,5248]{1,0:T(8,128)(2,1)S(1)} %join.3.here_ref, ...), custom_call_target="tpu_custom_call" | custom-call | tf_op jit(solution)/shard_map/layer/pallas_call | solution.py:347
  26.1 0.2 collective-permute-start.5
  26.3 1.3 %rest.1 = (f32[32,2560]{1,0:T(8,128)S(1)}, bf16[32,2560]{1,0:T(8,128)(2,1)S(1)}) custom-call(bf16[64,512]{1,0:T(8,128)(2,1)S(1)} %get-tuple-element.24.shared_hidden, bf16[64,512]{1,0:T(8,128)(2,1)S(1)} %get-tuple-element.25.cold_hidden, bf16[64,256]{1,0:T(8,128)(2,1)S(1)} %get-tuple-element.26.hot_hidden, f32[64,128]{1,0:T(8,128)S(1)} %get-tuple-element.27.gate_ref, ...), custom_call_target="tpu_custom_call" | custom-call | tf_op jit(solution)/shard_map/rest/pallas_call | solution.py:321
  27.5 0.4 %collective-permute-start.7 = (bf16[32,2560]{1,0:T(8,128)(2,1)S(1)}, bf16[32,2560]{1,0:T(8,128)(2,1)S(1)}, u32[]{:S(2)}, u32[]{:S(2)}) collective-permute-start(bf16[32,2560]{1,0:T(8,128)(2,1)S(1)} %get-tuple-element.30), channel_id=1, source_target_pairs={{0,1},{1,0},{2,3},{3,2},{4,5},{5,4},{6,7},{7,6},{8,9},{9,8},{10,11... | collective-permute-start | bytes 491528 | tf_op jit(solution)/shard_map/ppermute | solution.py:22
  28.0 0.0 collective-permute-done.5
  28.0 1.3 %collective-permute-start.6 = (bf16[16,2560]{1,0:T(8,128)(2,1)S(1)}, bf16[16,2560]{1,0:T(8,128)(2,1)S(1)}, u32[]{:S(2)}, u32[]{:S(2)}) collective-permute-start(bf16[16,2560]{1,0:T(8,128)(2,1)S(1)} %slice.67), channel_id=1, source_target_pairs={{0,2},{2,0},{4,6},{6,4},{8,10},{10,8},{12,14},{14,12},{1,3},{3,1},... | collective-permute-start | bytes 245768 | tf_op jit(solution)/shard_map/ppermute | solution.py:18
  29.3 0.0 collective-permute-done.7
  29.4 1.0 %collective-permute-start.8 = (bf16[16,2560]{1,0:T(8,128)(2,1)S(1)}, bf16[16,2560]{1,0:T(8,128)(2,1)S(1)}, u32[]{:S(2)}, u32[]{:S(2)}) collective-permute-start(bf16[16,2560]{1,0:T(8,128)(2,1)S(1)} %slice.66), channel_id=1, source_target_pairs={{0,2},{2,0},{4,6},{6,4},{8,10},{10,8},{12,14},{14,12},{1,3},{3,1},... | collective-permute-start | bytes 245768 | tf_op jit(solution)/shard_map/ppermute | solution.py:18
  30.4 2.8 %collective-permute-done.6 = bf16[16,2560]{1,0:T(8,128)(2,1)S(1)} collective-permute-done((bf16[16,2560]{1,0:T(8,128)(2,1)S(1)}, bf16[16,2560]{1,0:T(8,128)(2,1)S(1)}, u32[]{:S(2)}, u32[]{:S(2)}) %collective-permute-start.6) | collective-permute-done | bytes 81952 | tf_op jit(solution)/shard_map/ppermute | solution.py:18
  33.2 1.2 %collective-permute-done.8 = bf16[16,2560]{1,0:T(8,128)(2,1)S(1)} collective-permute-done((bf16[16,2560]{1,0:T(8,128)(2,1)S(1)}, bf16[16,2560]{1,0:T(8,128)(2,1)S(1)}, u32[]{:S(2)}, u32[]{:S(2)}) %collective-permute-start.8) | collective-permute-done | bytes 81952 | tf_op jit(solution)/shard_map/ppermute | solution.py:18
  34.4 0.1 fusion.6
  34.4 1.3 %collective-permute-start.9 = (bf16[4,5120]{1,0:T(4,128)(2,1)S(1)}, bf16[4,5120]{1,0:T(4,128)(2,1)S(1)}, u32[]{:S(2)}, u32[]{:S(2)}) collective-permute-start(bf16[4,5120]{1,0:T(4,128)(2,1)S(1)} %get-tuple-element.31), channel_id=1, source_target_pairs={{0,4},{2,6},{4,0},{6,2},{8,12},{10,14},{12,8},{14,10},{1,5},{3,7},... | collective-permute-start | bytes 122888 | tf_op jit(solution)/shard_map/ppermute | solution.py:18
  35.8 2.4 %collective-permute-start.11 = (bf16[4,5120]{1,0:T(4,128)(2,1)S(1)}, bf16[4,5120]{1,0:T(4,128)(2,1)S(1)}, u32[]{:S(2)}, u32[]{:S(2)}) collective-permute-start(bf16[4,5120]{1,0:T(4,128)(2,1)S(1)} %get-tuple-element.32), channel_id=1, source_target_pairs={{0,12},{2,14},{4,8},{6,10},{8,4},{10,6},{12,0},{14,2},{1,13},{3,15... | collective-permute-start | bytes 122888 | tf_op jit(solution)/shard_map/ppermute | solution.py:18
  38.2 0.5 %collective-permute-start.10 = (bf16[4,5120]{1,0:T(4,128)(2,1)S(1)}, bf16[4,5120]{1,0:T(4,128)(2,1)S(1)}, u32[]{:S(2)}, u32[]{:S(2)}) collective-permute-start(bf16[4,5120]{1,0:T(4,128)(2,1)S(1)} %get-tuple-element.33), channel_id=1, source_target_pairs={{0,8},{2,10},{4,12},{6,14},{8,0},{10,2},{12,4},{14,6},{1,9},{3,11}... | collective-permute-start | bytes 122888 | tf_op jit(solution)/shard_map/ppermute | solution.py:18
  38.7 0.0 collective-permute-done.9
  38.7 3.4 %collective-permute-done.11 = bf16[4,5120]{1,0:T(4,128)(2,1)S(1)} collective-permute-done((bf16[4,5120]{1,0:T(4,128)(2,1)S(1)}, bf16[4,5120]{1,0:T(4,128)(2,1)S(1)}, u32[]{:S(2)}, u32[]{:S(2)}) %collective-permute-start.11) | collective-permute-done | bytes 40992 | tf_op jit(solution)/shard_map/ppermute | solution.py:18
  42.1 1.0 %collective-permute-done.10 = bf16[4,5120]{1,0:T(4,128)(2,1)S(1)} collective-permute-done((bf16[4,5120]{1,0:T(4,128)(2,1)S(1)}, bf16[4,5120]{1,0:T(4,128)(2,1)S(1)}, u32[]{:S(2)}, u32[]{:S(2)}) %collective-permute-start.10) | collective-permute-done | bytes 40992 | tf_op jit(solution)/shard_map/ppermute | solution.py:18
  43.1 0.7 %fusion.5 = bf16[4,5120]{1,0:T(4,128)(2,1)} fusion(bf16[4,5120]{1,0:T(4,128)(2,1)S(1)} %collective-permute-done.11, bf16[4,5120]{1,0:T(4,128)(2,1)S(1)} %collective-permute-done.10, bf16[4,5120]{1,0:T(4,128)(2,1)S(1)} %collective-permute-done.9, f32[16,2560]{1,0:T(8,128)S(1)} %slice_add_fusion, f32[16,2560]{1,0:T(8,128)S(1)} %slice_add_fusion.1), kind=kLoop, calls=%fused_computation.14 | loop fusion | flops 163840 | bytes 491520 | tf_op jit(solution)/shard_map/convert_element_type | solution.py:419
  (11 shorter events, 0.2 us)
Async XLA Ops:
  1.5 17.6 %slice-start = ((s8[5242880]{0:T(1024)(128)(4,1)}), s8[4194304]{0:T(1024)(128)(4,1)S(1)}, s32[]{:S(2)}) async-start(s8[5242880]{0:T(1024)(128)(4,1)} %bitcast.6), calls=%async_computation | async-start | bytes 8388608
  1.5 17.6 %slice-start.2 = ((s8[5242880]{0:T(1024)(128)(4,1)}), s8[4194304]{0:T(1024)(128)(4,1)S(1)}, s32[]{:S(2)}) async-start(s8[5242880]{0:T(1024)(128)(4,1)} %bitcast.8), calls=%async_computation.2 | async-start | bytes 8388608
  1.6 9.9 %collective-permute-start.2 = (bf16[4,5248]{1,0:T(4,128)(2,1)S(1)}, bf16[4,5248]{1,0:T(4,128)(2,1)S(1)}, u32[]{:S(2)}, u32[]{:S(2)}) collective-permute-start(bf16[4,5248]{1,0:T(4,128)(2,1)S(1)} %pack.1.after_ref.refs_1_), channel_id=1, source_target_pairs={{0,12},{2,14},{4,8},{6,10},{8,4},{10,6},{12,0},{14,2},{1,13},{3,15... | collective-permute-start | bytes 125960 | tf_op jit(solution)/shard_map/ppermute | solution.py:18
  6.7 4.9 %collective-permute-start.1 = (bf16[4,5248]{1,0:T(4,128)(2,1)S(1)}, bf16[4,5248]{1,0:T(4,128)(2,1)S(1)}, u32[]{:S(2)}, u32[]{:S(2)}) collective-permute-start(bf16[4,5248]{1,0:T(4,128)(2,1)S(1)} %pack.1.after_ref.refs_1_), channel_id=1, source_target_pairs={{0,8},{2,10},{4,12},{6,14},{8,0},{10,2},{12,4},{14,6},{1,9},{3,11}... | collective-permute-start | bytes 125960 | tf_op jit(solution)/shard_map/ppermute | solution.py:18
  6.7 4.9 %collective-permute-start = (bf16[4,5248]{1,0:T(4,128)(2,1)S(1)}, bf16[4,5248]{1,0:T(4,128)(2,1)S(1)}, u32[]{:S(2)}, u32[]{:S(2)}) collective-permute-start(bf16[4,5248]{1,0:T(4,128)(2,1)S(1)} %pack.1.after_ref.refs_1_), channel_id=1, source_target_pairs={{0,4},{2,6},{4,0},{6,2},{8,12},{10,14},{12,8},{14,10},{1,5},{3,7},... | collective-permute-start | bytes 125960 | tf_op jit(solution)/shard_map/ppermute | solution.py:18
  11.6 7.5 %slice-start.1 = ((s8[5242880]{0:T(1024)(128)(4,1)}), s8[1048576]{0:T(1024)(128)(4,1)S(1)}, s32[]{:S(2)}) async-start(s8[5242880]{0:T(1024)(128)(4,1)} %bitcast.6), calls=%async_computation.1 | async-start | bytes 2097152
  11.6 7.5 %slice-start.3 = ((s8[5242880]{0:T(1024)(128)(4,1)}), s8[1048576]{0:T(1024)(128)(4,1)S(1)}, s32[]{:S(2)}) async-start(s8[5242880]{0:T(1024)(128)(4,1)} %bitcast.8), calls=%async_computation.3 | async-start | bytes 2097152
  11.7 5.7 %collective-permute-start.3 = (bf16[16,5248]{1,0:T(8,128)(2,1)S(1)}, bf16[16,5248]{1,0:T(8,128)(2,1)S(1)}, u32[]{:S(2)}, u32[]{:S(2)}) collective-permute-start(bf16[16,5248]{1,0:T(8,128)(2,1)S(1)} %join.2.after_ref.refs_1_), channel_id=1, source_target_pairs={{0,2},{2,0},{4,6},{6,4},{8,10},{10,8},{12,14},{14,12},{1,3},{3,1},... | collective-permute-start | bytes 503816 | tf_op jit(solution)/shard_map/ppermute | solution.py:18
  17.4 1.7 %collective-permute-start.4 = (bf16[32,5248]{1,0:T(8,128)(2,1)S(1)}, bf16[32,5248]{1,0:T(8,128)(2,1)S(1)}, u32[]{:S(2)}, u32[]{:S(2)}) collective-permute-start(bf16[32,5248]{1,0:T(8,128)(2,1)S(1)} %join.3.here_ref), channel_id=1, source_target_pairs={{0,1},{1,0},{2,3},{3,2},{4,5},{5,4},{6,7},{7,6},{8,9},{9,8},{10,11... | collective-permute-start | bytes 1007624 | tf_op jit(solution)/shard_map/ppermute | solution.py:22
  26.1 1.9 %collective-permute-start.5 = (bf16[32,2560]{1,0:T(8,128)(2,1)S(1)}, bf16[32,2560]{1,0:T(8,128)(2,1)S(1)}, u32[]{:S(2)}, u32[]{:S(2)}) collective-permute-start(bf16[32,2560]{1,0:T(8,128)(2,1)S(1)} %get-tuple-element.23), channel_id=1, source_target_pairs={{0,1},{1,0},{2,3},{3,2},{4,5},{5,4},{6,7},{7,6},{8,9},{9,8},{10,11... | collective-permute-start | bytes 491528 | tf_op jit(solution)/shard_map/ppermute | solution.py:22
  27.5 1.8 %collective-permute-start.7 = (bf16[32,2560]{1,0:T(8,128)(2,1)S(1)}, bf16[32,2560]{1,0:T(8,128)(2,1)S(1)}, u32[]{:S(2)}, u32[]{:S(2)}) collective-permute-start(bf16[32,2560]{1,0:T(8,128)(2,1)S(1)} %get-tuple-element.30), channel_id=1, source_target_pairs={{0,1},{1,0},{2,3},{3,2},{4,5},{5,4},{6,7},{7,6},{8,9},{9,8},{10,11... | collective-permute-start | bytes 491528 | tf_op jit(solution)/shard_map/ppermute | solution.py:22
  28.0 5.1 %collective-permute-start.6 = (bf16[16,2560]{1,0:T(8,128)(2,1)S(1)}, bf16[16,2560]{1,0:T(8,128)(2,1)S(1)}, u32[]{:S(2)}, u32[]{:S(2)}) collective-permute-start(bf16[16,2560]{1,0:T(8,128)(2,1)S(1)} %slice.67), channel_id=1, source_target_pairs={{0,2},{2,0},{4,6},{6,4},{8,10},{10,8},{12,14},{14,12},{1,3},{3,1},... | collective-permute-start | bytes 245768 | tf_op jit(solution)/shard_map/ppermute | solution.py:18
  29.4 4.9 %collective-permute-start.8 = (bf16[16,2560]{1,0:T(8,128)(2,1)S(1)}, bf16[16,2560]{1,0:T(8,128)(2,1)S(1)}, u32[]{:S(2)}, u32[]{:S(2)}) collective-permute-start(bf16[16,2560]{1,0:T(8,128)(2,1)S(1)} %slice.66), channel_id=1, source_target_pairs={{0,2},{2,0},{4,6},{6,4},{8,10},{10,8},{12,14},{14,12},{1,3},{3,1},... | collective-permute-start | bytes 245768 | tf_op jit(solution)/shard_map/ppermute | solution.py:18
  34.4 4.2 %collective-permute-start.9 = (bf16[4,5120]{1,0:T(4,128)(2,1)S(1)}, bf16[4,5120]{1,0:T(4,128)(2,1)S(1)}, u32[]{:S(2)}, u32[]{:S(2)}) collective-permute-start(bf16[4,5120]{1,0:T(4,128)(2,1)S(1)} %get-tuple-element.31), channel_id=1, source_target_pairs={{0,4},{2,6},{4,0},{6,2},{8,12},{10,14},{12,8},{14,10},{1,5},{3,7},... | collective-permute-start | bytes 122888 | tf_op jit(solution)/shard_map/ppermute | solution.py:18
  35.8 6.3 %collective-permute-start.11 = (bf16[4,5120]{1,0:T(4,128)(2,1)S(1)}, bf16[4,5120]{1,0:T(4,128)(2,1)S(1)}, u32[]{:S(2)}, u32[]{:S(2)}) collective-permute-start(bf16[4,5120]{1,0:T(4,128)(2,1)S(1)} %get-tuple-element.32), channel_id=1, source_target_pairs={{0,12},{2,14},{4,8},{6,10},{8,4},{10,6},{12,0},{14,2},{1,13},{3,15... | collective-permute-start | bytes 122888 | tf_op jit(solution)/shard_map/ppermute | solution.py:18
  38.2 4.9 %collective-permute-start.10 = (bf16[4,5120]{1,0:T(4,128)(2,1)S(1)}, bf16[4,5120]{1,0:T(4,128)(2,1)S(1)}, u32[]{:S(2)}, u32[]{:S(2)}) collective-permute-start(bf16[4,5120]{1,0:T(4,128)(2,1)S(1)} %get-tuple-element.33), channel_id=1, source_target_pairs={{0,8},{2,10},{4,12},{6,14},{8,0},{10,2},{12,4},{14,6},{1,9},{3,11}... | collective-permute-start | bytes 122888 | tf_op jit(solution)/shard_map/ppermute | solution.py:18
